TPU v7x, 128 devices: a whole 4x4x4 slice. The times are simulated.
128 devices in a mesh: bx: 8 (over y, core), by: 16 (over z, x).
Axes of the slice: x: 4, y: 4, z: 4, core: 2. Of those that a mesh axis runs over, the one named last changes fastest.
Arguments:
- features: bfloat16 [64, 128, 256, 128], P(None, 'bx', 'by'), may hold values from -6 to 6
- labels: int32 [128, 256, 128], P('bx', 'by'), may hold values from 0 to 255, as said below
- conv_weight: bfloat16 [64, 1728], replicated, may hold values from -0.15625 to 0.15625
- conv_bias: float32 [64], replicated, may hold values from -3 to 3
- head_weight: bfloat16 [3, 64], replicated, may hold values from -0.75 to 0.75
- head_bias: float32 [3], replicated, may hold values from -3 to 3
- edge_ends: int32 [128, 2, 512], P(('bx', 'by')), may hold values from 0 to 255
- edge_owner: int32 [128, 512, 1], P(('bx', 'by')), may hold values from 0 to 127; in each aligned block of 512 rows (0 to 511, 512 to 1023, ..., all dimensions but the last counted through in order) at most 8 rows name the same one
- edge_row: int32 [128, 512], P(('bx', 'by')), may hold values from 0 to 127
- edge_count: int32 [128], P(('bx', 'by')), may hold values from 128 to 512, as said below
Outputs:
- edge_weight: float32 [16384], P(('bx', 'by'))
Inputs may be any that keep to these rules, and one draw needn't show every extreme that they name: `labels`: supervoxels are spatially coherent regions. `edge_owner`: no owner is named by more than 8 of one brick's 512 slots, a bound that some block reaches. `edge_count`: some brick has all 512 slots live.
All inputs are finite; a program needn't handle non-finite values.
Results may differ from a plain program's by a relative error of at most 0.0003.
Values may be sent and summed in bfloat16 or wider, within the bound.
A program may use at most 128 MiB of HBM per device.

v0:
```python
import jax
import jax.numpy as jnp
from jax import lax
from jax.sharding import PartitionSpec as P

LABELS = 256
EO = 128


def padded_2(cells, sides, width):
    for axis, dim in sides:
        count = lax.axis_size(axis)
        ends = count - 1
        head = lax.slice_in_dim(cells, 0, width, axis=dim)
        tail = lax.slice_in_dim(cells, cells.shape[dim] - width, cells.shape[dim], axis=dim)
        cells = jnp.concatenate(
            [
                lax.ppermute(tail, axis, [(i, (i + 1) % count) for i in range(ends)]),
                cells,
                lax.ppermute(head, axis, [((i + 1) % count, i) for i in range(ends)]),
            ],
            axis=dim,
        )
    return cells


def from_behind(value, axis, steps):
    count = lax.axis_size(axis)
    leading, last = (max(0, -steps), min(count, count - steps))
    return lax.ppermute(value, axis, [(source, source + steps) for source in range(leading, last)])


def brick_sums(
    padded,
    labels,
    below_x,
    below_y,
    below_z,
    conv_weight,
    conv_bias,
    head_weight,
    head_bias,
    ends,
    live,
):
    chans = padded.shape[0]
    planes = labels.shape[0]
    rows = labels.shape[1]
    depth = labels.shape[2]
    label_ids = jnp.arange(LABELS, dtype=jnp.int32)
    stride = 4
    width = stride * rows * depth

    def one_block(start):
        block = lax.dynamic_slice_in_dim(padded, start, stride + 2, 1)
        pre = jnp.zeros((chans, width), jnp.float32) + conv_bias[:, None]
        for dx in range(3):
            for dy in range(3):
                for dz in range(3):
                    tap = 9 * dx + 3 * dy + dz
                    piece = block[:, dx : dx + stride, dy : dy + rows, dz : dz + depth].reshape(
                        chans, width
                    )
                    weight_tap = conv_weight[:, tap * chans : (tap + 1) * chans]
                    pre = pre + jnp.dot(weight_tap, piece, preferred_element_type=jnp.float32)
        hidden = jnp.maximum(pre, 0.0).astype(jnp.bfloat16)
        logits = (
            jnp.dot(head_weight, hidden, preferred_element_type=jnp.float32) + head_bias[:, None]
        )
        affin = jax.nn.sigmoid(logits).astype(jnp.bfloat16).reshape(-1)
        own = lax.dynamic_slice_in_dim(labels, start, stride, 0).reshape(-1)
        others = jnp.concatenate(
            [
                lax.dynamic_slice_in_dim(neighbour, start, stride, 0).reshape(-1)
                for neighbour in (below_x, below_y, below_z)
            ],
            0,
        )
        owns = jnp.concatenate([own, own, own], 0)
        left = (owns[:, None] == label_ids[None, :]).astype(jnp.bfloat16)
        right = jnp.where(others[:, None] == label_ids[None, :], affin[:, None], jnp.bfloat16(0.0))
        return lax.dot_general(
            left, right, (((0,), (0,)), ((), ())), preferred_element_type=jnp.float32
        )

    starts = jnp.arange(0, planes, stride, dtype=jnp.int32)
    pair_table = jnp.sum(lax.map(one_block, starts), axis=0)
    keep = 1.0 - jnp.eye(LABELS, dtype=jnp.float32)
    symmetric = ((pair_table + pair_table.T) * keep).reshape(-1)
    return symmetric[ends[0] * LABELS + ends[1]] * live


def on_device(
    features,
    labels,
    conv_weight,
    conv_bias,
    head_weight,
    head_bias,
    edge_ends,
    edge_owner,
    edge_row,
    edge_count,
):
    widened = padded_2(features, (("bx", 1), ("by", 2)), 1)
    padded = jnp.pad(widened, ((0, 0), (0, 0), (0, 0), (1, 1)))
    raised = labels + 1
    plane = from_behind(raised[-1:], "bx", 1) - 1
    edge_line = from_behind(raised[:, -1:], "by", 1) - 1
    below_x = jnp.concatenate([plane, labels[:-1]], axis=0)
    below_y = jnp.concatenate([edge_line, labels[:, :-1]], axis=1)
    outside = jnp.full((labels.shape[0], labels.shape[1], 1), -1, jnp.int32)
    below_z = jnp.concatenate([outside, labels[:, :, :-1]], axis=2)
    ends = edge_ends[0]
    owners = edge_owner[0, :, 0]
    targets = edge_row[0]
    slots = ends.shape[1]
    live = (jnp.arange(slots, dtype=jnp.int32) < edge_count[0]).astype(jnp.float32)
    partial_value = brick_sums(
        padded,
        labels,
        below_x,
        below_y,
        below_z,
        conv_weight,
        conv_bias,
        head_weight,
        head_bias,
        ends,
        live,
    )
    devices = lax.axis_size(("bx", "by"))
    spread = jnp.zeros((devices * EO,), jnp.float32).at[owners * EO + targets].add(partial_value)
    return lax.psum_scatter(spread, ("bx", "by"), scatter_dimension=0, tiled=True)


def solution(mesh):
    placed = (
        P(None, "bx", "by", None),
        P("bx", "by", None),
        P(),
        P(),
        P(),
        P(),
        P(("bx", "by"), None, None),
        P(("bx", "by"), None, None),
        P(("bx", "by"), None),
        P(("bx", "by")),
    )
    return jax.shard_map(
        on_device, mesh=mesh, in_specs=placed, out_specs=P(("bx", "by")), check_vma=False
    )
```

profile of v0, /device:TPU:1, one launch (start us, length us, event | category | flops | bytes accessed | tf_op | source)
XLA Modules:
  0.0 757.4 jit_solution(18124611249400438742)
XLA Ops:
  7.8 4.6 collective-permute-start.2
  12.5 1.9 collective-permute-start.3
  14.4 3.6 collective-permute-start
  18.1 3.1 collective-permute-start.1
  24.6 5.2 constant_dynamic-update-slice_fusion.1
  29.8 3.1 collective-permute-start.4
  35.0 4.3 collective-permute-done.4
  39.3 4.2 collective-permute-done.5
  43.5 8.7 %fusion.127 = bf16[64,18,18,130]{3,0,2,1:T(8,128)(2,1)} fusion(bf16[64,18,1,128]{3,0,2,1:T(8,128)(2,1)S(1)} %collective-permute-done.5, bf16[64,18,16,128]{3,0,2,1:T(8,128)(2,1)S(1)} %constant_dynamic-update-slice_fusion, bf16[64,18,1,128]{3,0,2,1:T(8,128)(2,1)S(1)} %collective-permute-done.4), kind=kLoop, calls=%fused_computation.185 | loop fusion | flops 32348160 | bytes 10699776 | tf_op jit(solution)/shard_map/concatenate | solution.py:16
  52.2 546.1 %while.12 = (s32[]{:T(128)}, f32[4,256,256]{2,1,0:T(8,128)}, s32[4]{0:T(128)S(1)}, s32[16,16,128]{2,1,0:T(8,128)S(1)}, s32[16,16,128]{2,1,0:T(8,128)}, /*index=5...) while((s32[]{:T(128)}, f32[4,256,256]{2,1,0:T(8,128)}, ...), condition=%wide.region_1.2_spmd.clone.clone, body=%wide.region_0.1_spmd.clone.clone.sunk | while | flops 5070610432 | bytes 304040160 | solution.py:87
  55.0 25.6 %constant_dynamic-slice_fusion.36 = (bf16[64,4,16,128]{3,0,2,1:T(8,128)(2,1)S(1)}, bf16[64,4,16,128]{3,0,2,1:T(8,128)(2,1)S(1)}, bf16[64,4,16,128]{3,0,2,1:T(8,1...) fusion(bf16[64,18,18,130]{3,0,2,1:T(8,128)(2,1)} %get-tuple-ele, ...), kind=kLoop, calls=%fused_computation.171.clone.1 | loop fusion | bytes 56623124 | tf_op jit(solution)/shard_map/while/body/eval_jaxpr/slice | solution.py:61
  80.6 1.9 copy.272
  84.5 1.7 convolution_add_fusion.33
  86.9 1.7 convolution_add_fusion.34
  89.3 1.7 convolution_add_fusion.35
  91.7 1.7 convolution_add_fusion.36
  94.2 1.7 convolution_add_fusion.37
  96.6 1.7 convolution_add_fusion.38
  99.1 1.7 convolution_add_fusion.39
  102.1 1.7 convolution_add_fusion.40
  138.3 1.8 fusion.268
  143.1 11.1 %iota_compare_fusion.16 = pred[24576,256]{1,0:T(32,128)(4,1)S(1)} fusion(s32[24576]{0:T(1024)S(1)} %pad_add_fusion.7), kind=kLoop, calls=%fused_computation.4.clone.clone.clone.clone.clone.clone.2.clone.1 | loop fusion | flops 6291456 | bytes 6389760 | tf_op jit(solution)/shard_map/while/body/eval_jaxpr/dot_general | solution.py:82
  154.3 33.5 %fusion.269 = f32[4,256,256]{2,1,0:T(8,128)} fusion(f32[4,256,256]{2,1,0:T(8,128)} %get-tuple-element.357, s32[]{:T(128)} %get-tuple-element.356, s32[24576]{0:T(1024)S(1)} %pad_add_fusion.6, bf16[24576]{0:T(1024)(128)(2,1)S(1)} %broadcast_in_dim.72, pred[24576,256]{1,0:T(32,128)(4,1)S(1)} %iota_compare_fusion.16), kind=kOutput, calls=%fused_computation.60.clone.3 | convolution fusion | flops 3233808384 | bytes 6701568 | tf_op jit(solution)/shard_map/while/body/eval_jaxpr/dot_general | solution.py:82
  190.7 26.0 %constant_dynamic-slice_fusion.36 = (bf16[64,4,16,128]{3,0,2,1:T(8,128)(2,1)S(1)}, bf16[64,4,16,128]{3,0,2,1:T(8,128)(2,1)S(1)}, bf16[64,4,16,128]{3,0,2,1:T(8,1...) fusion(bf16[64,18,18,130]{3,0,2,1:T(8,128)(2,1)} %get-tuple-ele, ...), kind=kLoop, calls=%fused_computation.171.clone.1 | loop fusion | bytes 56623124 | tf_op jit(solution)/shard_map/while/body/eval_jaxpr/slice | solution.py:61
  216.7 1.9 copy.272
  220.6 1.7 convolution_add_fusion.33
  223.0 1.7 convolution_add_fusion.34
  225.4 1.7 convolution_add_fusion.35
  227.9 1.7 convolution_add_fusion.36
  230.3 1.7 convolution_add_fusion.37
  232.7 1.7 convolution_add_fusion.38
  235.2 1.7 convolution_add_fusion.39
  237.8 1.7 convolution_add_fusion.40
  274.3 1.8 fusion.268
  279.1 11.1 %iota_compare_fusion.16 = pred[24576,256]{1,0:T(32,128)(4,1)S(1)} fusion(s32[24576]{0:T(1024)S(1)} %pad_add_fusion.7), kind=kLoop, calls=%fused_computation.4.clone.clone.clone.clone.clone.clone.2.clone.1 | loop fusion | flops 6291456 | bytes 6389760 | tf_op jit(solution)/shard_map/while/body/eval_jaxpr/dot_general | solution.py:82
  290.2 33.5 %fusion.269 = f32[4,256,256]{2,1,0:T(8,128)} fusion(f32[4,256,256]{2,1,0:T(8,128)} %get-tuple-element.357, s32[]{:T(128)} %get-tuple-element.356, s32[24576]{0:T(1024)S(1)} %pad_add_fusion.6, bf16[24576]{0:T(1024)(128)(2,1)S(1)} %broadcast_in_dim.72, pred[24576,256]{1,0:T(32,128)(4,1)S(1)} %iota_compare_fusion.16), kind=kOutput, calls=%fused_computation.60.clone.3 | convolution fusion | flops 3233808384 | bytes 6701568 | tf_op jit(solution)/shard_map/while/body/eval_jaxpr/dot_general | solution.py:82
  326.4 26.1 %constant_dynamic-slice_fusion.36 = (bf16[64,4,16,128]{3,0,2,1:T(8,128)(2,1)S(1)}, bf16[64,4,16,128]{3,0,2,1:T(8,128)(2,1)S(1)}, bf16[64,4,16,128]{3,0,2,1:T(8,1...) fusion(bf16[64,18,18,130]{3,0,2,1:T(8,128)(2,1)} %get-tuple-ele, ...), kind=kLoop, calls=%fused_computation.171.clone.1 | loop fusion | bytes 56623124 | tf_op jit(solution)/shard_map/while/body/eval_jaxpr/slice | solution.py:61
  352.5 1.9 copy.272
  358.8 1.7 convolution_add_fusion.34
  361.2 1.7 convolution_add_fusion.35
  363.7 1.7 convolution_add_fusion.36
  366.1 1.7 convolution_add_fusion.37
  368.5 1.7 convolution_add_fusion.38
  371.0 1.7 convolution_add_fusion.39
  373.8 1.7 convolution_add_fusion.40
  410.1 1.8 fusion.268
  414.9 11.1 %iota_compare_fusion.16 = pred[24576,256]{1,0:T(32,128)(4,1)S(1)} fusion(s32[24576]{0:T(1024)S(1)} %pad_add_fusion.7), kind=kLoop, calls=%fused_computation.4.clone.clone.clone.clone.clone.clone.2.clone.1 | loop fusion | flops 6291456 | bytes 6389760 | tf_op jit(solution)/shard_map/while/body/eval_jaxpr/dot_general | solution.py:82
  426.0 33.5 %fusion.269 = f32[4,256,256]{2,1,0:T(8,128)} fusion(f32[4,256,256]{2,1,0:T(8,128)} %get-tuple-element.357, s32[]{:T(128)} %get-tuple-element.356, s32[24576]{0:T(1024)S(1)} %pad_add_fusion.6, bf16[24576]{0:T(1024)(128)(2,1)S(1)} %broadcast_in_dim.72, pred[24576,256]{1,0:T(32,128)(4,1)S(1)} %iota_compare_fusion.16), kind=kOutput, calls=%fused_computation.60.clone.3 | convolution fusion | flops 3233808384 | bytes 6701568 | tf_op jit(solution)/shard_map/while/body/eval_jaxpr/dot_general | solution.py:82
  462.4 26.6 %constant_dynamic-slice_fusion.36 = (bf16[64,4,16,128]{3,0,2,1:T(8,128)(2,1)S(1)}, bf16[64,4,16,128]{3,0,2,1:T(8,128)(2,1)S(1)}, bf16[64,4,16,128]{3,0,2,1:T(8,1...) fusion(bf16[64,18,18,130]{3,0,2,1:T(8,128)(2,1)} %get-tuple-ele, ...), kind=kLoop, calls=%fused_computation.171.clone.1 | loop fusion | bytes 56623124 | tf_op jit(solution)/shard_map/while/body/eval_jaxpr/slice | solution.py:61
  489.0 1.9 copy.272
  492.9 1.7 convolution_add_fusion.33
  495.3 1.7 convolution_add_fusion.34
  497.8 1.7 convolution_add_fusion.35
  500.2 1.7 convolution_add_fusion.36
  502.6 1.7 convolution_add_fusion.37
  505.1 1.7 convolution_add_fusion.38
  507.5 1.7 convolution_add_fusion.39
  510.1 1.7 convolution_add_fusion.40
  546.6 1.8 fusion.268
  551.4 11.1 %iota_compare_fusion.16 = pred[24576,256]{1,0:T(32,128)(4,1)S(1)} fusion(s32[24576]{0:T(1024)S(1)} %pad_add_fusion.7), kind=kLoop, calls=%fused_computation.4.clone.clone.clone.clone.clone.clone.2.clone.1 | loop fusion | flops 6291456 | bytes 6389760 | tf_op jit(solution)/shard_map/while/body/eval_jaxpr/dot_general | solution.py:82
  562.5 33.5 %fusion.269 = f32[4,256,256]{2,1,0:T(8,128)} fusion(f32[4,256,256]{2,1,0:T(8,128)} %get-tuple-element.357, s32[]{:T(128)} %get-tuple-element.356, s32[24576]{0:T(1024)S(1)} %pad_add_fusion.6, bf16[24576]{0:T(1024)(128)(2,1)S(1)} %broadcast_in_dim.72, pred[24576,256]{1,0:T(32,128)(4,1)S(1)} %iota_compare_fusion.16), kind=kOutput, calls=%fused_computation.60.clone.3 | convolution fusion | flops 3233808384 | bytes 6701568 | tf_op jit(solution)/shard_map/while/body/eval_jaxpr/dot_general | solution.py:82
  600.0 3.1 gather_fusion
  603.1 4.0 scatter_custom_fusion
  607.1 141.9 %all-reduce.5.cloned.1.call-done = f32[16384]{0:T(1024)} async-done(((f32[16384]{0:T(1024)}), f32[16384]{0:T(1024)}) %all-reduce.5.cloned.1.call-update) | async-done | bytes 65552
  (354 shorter events, 186.0 us)
Async XLA Ops:
  6.5 7.9 %copy-start.10 = (s32[16,16,128]{2,1,0:T(8,128)S(1)}, s32[16,16,128]{2,1,0:T(8,128)}, u32[]{:S(2)}) copy-start(s32[16,16,128]{2,1,0:T(8,128)} %param.13) | copy-start | bytes 393220
  6.5 14.7 %copy-start.14 = (s32[1,2,512]{2,1,0:T(2,128)S(1)}, s32[1,2,512]{2,1,0:T(2,128)}, u32[]{:S(2)}) copy-start(s32[1,2,512]{2,1,0:T(2,128)} %param.18) | copy-start | bytes 12292
  6.5 15.3 %copy-start.16 = (s32[1,512,1]{1,2,0:T(1,128)S(1)}, s32[1,512,1]{1,2,0:T(1,128)}, u32[]{:S(2)}) copy-start(s32[1,512,1]{1,2,0:T(1,128)} %param.19) | copy-start | bytes 6148
  6.5 15.3 %copy-start.15 = (s32[1,512]{1,0:T(1,128)S(1)}, s32[1,512]{1,0:T(1,128)}, u32[]{:S(2)}) copy-start(s32[1,512]{1,0:T(1,128)} %param.20) | copy-start | bytes 6148
  6.5 742.5 %all-reduce.5.cloned.1.call-start = ((), (), s32[]{:S(2)}) async-start(), calls=%async_computation | async-start | bytes 131072
  7.8 16.8 %collective-permute-start.2 = (bf16[64,1,16,128]{3,0,2,1:T(8,128)(2,1)S(1)}, bf16[64,1,16,128]{3,0,2,1:T(8,128)(2,1)S(1)}, u32[]{:S(2)}, u32[]{:S(2)}) collective-permute-start(bf16[64,1,16,128]{3,0,2,1:T(8,128)(2,1)S(1)} %copy.184), channel_id=1, source_target_pairs={{0,16},{16,32},{32,48},{48,64},{64,80},{80,96},{96,112},{1,17},{17... | collective-permute-start | bytes 786440 | tf_op jit(solution)/shard_map/ppermute | solution.py:18
  12.5 17.3 %collective-permute-start.3 = (bf16[64,1,16,128]{3,0,2,1:T(8,128)(2,1)S(1)}, bf16[64,1,16,128]{3,0,2,1:T(8,128)(2,1)S(1)}, u32[]{:S(2)}, u32[]{:S(2)}) collective-permute-start(bf16[64,1,16,128]{3,0,2,1:T(8,128)(2,1)S(1)} %copy.185), channel_id=1, source_target_pairs={{16,0},{32,16},{48,32},{64,48},{80,64},{96,80},{112,96},{17,1},{33... | collective-permute-start | bytes 786440 | tf_op jit(solution)/shard_map/ppermute | solution.py:20
  14.4 9.4 %collective-permute-start = (s32[1,16,128]{2,1,0:T(8,128)S(1)}, s32[1,16,128]{2,1,0:T(8,128)S(1)}, u32[]{:S(2)}, u32[]{:S(2)}) collective-permute-start(s32[1,16,128]{2,1,0:T(8,128)S(1)} %slice.318), channel_id=1, source_target_pairs={{0,16},{16,32},{32,48},{48,64},{64,80},{80,96},{96,112},{1,17},{17... | collective-permute-start | bytes 24584 | tf_op jit(solution)/shard_map/ppermute | solution.py:30
  18.1 16.2 %collective-permute-start.1 = (s32[16,1,128]{2,1,0:T(1,128)S(1)}, s32[16,1,128]{2,1,0:T(1,128)S(1)}, u32[]{:S(2)}, u32[]{:S(2)}) collective-permute-start(s32[16,1,128]{2,1,0:T(1,128)S(1)} %slice.319), channel_id=1, source_target_pairs={{0,1},{1,2},{2,3},{3,4},{4,5},{5,6},{6,7},{7,8},{8,9},{9,10},{10,1... | collective-permute-start | bytes 24584 | tf_op jit(solution)/shard_map/ppermute | solution.py:30
  29.8 9.4 %collective-permute-start.4 = (bf16[64,18,1,128]{3,0,2,1:T(8,128)(2,1)S(1)}, bf16[64,18,1,128]{3,0,2,1:T(8,128)(2,1)S(1)}, u32[]{:S(2)}, u32[]{:S(2)}) collective-permute-start(bf16[64,18,1,128]{3,0,2,1:T(8,128)(2,1)S(1)} %get-tuple-element.199), channel_id=1, source_target_pairs={{0,1},{1,2},{2,3},{3,4},{4,5},{5,6},{6,7},{7,8},{8,9},{9,10},{10,1... | collective-permute-start | bytes 884744 | tf_op jit(solution)/shard_map/ppermute | solution.py:18
  33.0 10.5 %collective-permute-start.5 = (bf16[64,18,1,128]{3,0,2,1:T(8,128)(2,1)S(1)}, bf16[64,18,1,128]{3,0,2,1:T(8,128)(2,1)S(1)}, u32[]{:S(2)}, u32[]{:S(2)}) collective-permute-start(bf16[64,18,1,128]{3,0,2,1:T(8,128)(2,1)S(1)} %get-tuple-element.200), channel_id=1, source_target_pairs={{1,0},{2,1},{3,2},{4,3},{5,4},{6,5},{7,6},{8,7},{9,8},{10,9},{11,1... | collective-permute-start | bytes 884744 | tf_op jit(solution)/shard_map/ppermute | solution.py:20
  35.0 17.2 %copy-start.12 = (f32[64]{0:T(128)S(1)}, f32[64]{0:T(128)}, u32[]{:S(2)}) copy-start(f32[64]{0:T(128)} %param.15) | copy-start | bytes 772
  35.0 17.2 %copy-start.17 = (bf16[3,64]{1,0:T(4,128)(2,1)S(1)}, bf16[3,64]{1,0:T(4,128)(2,1)}, u32[]{:S(2)}) copy-start(bf16[3,64]{1,0:T(4,128)(2,1)} %param.16) | copy-start | bytes 1156
  35.0 17.2 %copy-start.18 = (f32[3]{0:T(128)S(1)}, f32[3]{0:T(128)}, u32[]{:S(2)}) copy-start(f32[3]{0:T(128)} %param.17) | copy-start | bytes 40
  52.4 2.5 copy-start.19
  80.6 2.0 copy-start.9
  84.4 1.7 copy-start.7
  86.9 1.8 copy-start.6
  89.3 1.7 copy-start.5
  91.7 1.8 copy-start.4
  94.2 1.7 copy-start.3
  96.6 1.7 copy-start.2
  99.1 1.7 copy-start.1
  102.1 1.8 copy-start
  154.2 33.5 %copy-start.11 = (s32[16,16,128]{2,1,0:T(8,128)S(1)}, s32[16,16,128]{2,1,0:T(8,128)}, u32[]{:S(2)}) copy-start(s32[16,16,128]{2,1,0:T(8,128)} %get-tuple-element.411) | copy-start | bytes 393220 | tf_op jit(solution)/shard_map/while
  154.3 33.5 %copy-start.20 = (s32[4]{0:T(128)S(1)}, s32[4]{0:T(128)}, u32[]{:S(2)}) copy-start(s32[4]{0:T(128)} %copy-done.19) | copy-start | bytes 52 | tf_op jit(solution)/shard_map/while
  188.2 2.5 copy-start.19
  216.7 2.0 copy-start.9
  218.6 1.2 copy-start.8
  220.6 1.7 copy-start.7
  223.0 1.8 copy-start.6
  225.4 1.7 copy-start.5
  227.9 1.7 copy-start.4
  230.3 1.7 copy-start.3
  232.7 1.8 copy-start.2
  235.2 1.7 copy-start.1
  237.8 1.8 copy-start
  290.2 33.5 %copy-start.11 = (s32[16,16,128]{2,1,0:T(8,128)S(1)}, s32[16,16,128]{2,1,0:T(8,128)}, u32[]{:S(2)}) copy-start(s32[16,16,128]{2,1,0:T(8,128)} %get-tuple-element.411) | copy-start | bytes 393220 | tf_op jit(solution)/shard_map/while
  290.2 33.5 %copy-start.20 = (s32[4]{0:T(128)S(1)}, s32[4]{0:T(128)}, u32[]{:S(2)}) copy-start(s32[4]{0:T(128)} %copy-done.19) | copy-start | bytes 52 | tf_op jit(solution)/shard_map/while
  323.9 2.5 copy-start.19
  352.5 2.0 copy-start.9
  356.4 1.7 copy-start.7
  358.8 1.8 copy-start.6
  361.2 1.7 copy-start.5
  363.7 1.7 copy-start.4
  366.1 1.7 copy-start.3
  368.5 1.8 copy-start.2
  371.0 1.7 copy-start.1
  373.8 1.8 copy-start
  426.0 33.5 %copy-start.11 = (s32[16,16,128]{2,1,0:T(8,128)S(1)}, s32[16,16,128]{2,1,0:T(8,128)}, u32[]{:S(2)}) copy-start(s32[16,16,128]{2,1,0:T(8,128)} %get-tuple-element.411) | copy-start | bytes 393220 | tf_op jit(solution)/shard_map/while
  426.0 33.5 %copy-start.20 = (s32[4]{0:T(128)S(1)}, s32[4]{0:T(128)}, u32[]{:S(2)}) copy-start(s32[4]{0:T(128)} %copy-done.19) | copy-start | bytes 52 | tf_op jit(solution)/shard_map/while
  459.9 2.5 copy-start.19
  489.0 2.0 copy-start.9
  492.9 1.7 copy-start.7
  495.3 1.8 copy-start.6
  497.7 1.7 copy-start.5
  500.2 1.7 copy-start.4
  502.6 1.7 copy-start.3
  505.0 1.8 copy-start.2
  507.5 1.7 copy-start.1
  510.1 1.8 copy-start
  562.5 33.5 %copy-start.11 = (s32[16,16,128]{2,1,0:T(8,128)S(1)}, s32[16,16,128]{2,1,0:T(8,128)}, u32[]{:S(2)}) copy-start(s32[16,16,128]{2,1,0:T(8,128)} %get-tuple-element.411) | copy-start | bytes 393220 | tf_op jit(solution)/shard_map/while
  562.5 33.5 %copy-start.20 = (s32[4]{0:T(128)S(1)}, s32[4]{0:T(128)}, u32[]{:S(2)}) copy-start(s32[4]{0:T(128)} %copy-done.19) | copy-start | bytes 52 | tf_op jit(solution)/shard_map/while
  598.3 1.7 copy-start.13
  (3 other events, 3.7 us)
Sparse Core Ops, SparseCore 0:
  607.2 141.7 all-reduce.4
where the time goes:
time: 766 us; the launch traced here: 757 us
  matrix products  287 us (37%)
  local copies, waits for them, and re-layouts  209 us (27%)
  waiting for transfers between devices  150 us (20%)
  other arithmetic  61 us (8%)
  starting transfers between devices  17.7 us (2%)
  loops' own time  17.7 us (2%)
  between operations  14.5 us (2%)
    dot_general x104, matrix products, one_block(): pre = pre + jnp.dot(weight_tap, piece, preferred_element_type=jnp.float32)  146 us
    unnamed x2, waiting for transfers between devices  142 us
    dot_general x4, matrix products, one_block(): lax.dot_general(left, right, (((0,), (0,)), ((), ())), preferred_element_...  134 us
    slice x4, local copies, waits for them, and re-layouts, one_block(): block[:, dx:dx + stride, dy:dy + rows, dz:dz + depth].reshape(chans, width)  104 us
    while x212, local copies, waits for them, and re-layouts  83.2 us
    dot_general x4, other arithmetic, one_block(): lax.dot_general(left, right, (((0,), (0,)), ((), ())), preferred_element_...  44.3 us
    another operation x1, loops' own time, brick_sums(): pair_table = jnp.sum(lax.map(one_block, starts), axis=0)  17.7 us
  transfers between devices with their start and end apart: 7, of which 3 were waited for; matrix products, arithmetic and copies ran while one was open for 1% of the time, Pallas kernels for 0%

commit v1 on v0

v1 whole, which is shorter than its diff:
```python
import functools

import jax
import jax.numpy as jnp
from jax import lax
from jax.experimental import pallas as pl
from jax.experimental.pallas import tpu as pltpu
from jax.sharding import PartitionSpec as P

LABELS = 256
EO = 128
NBX = 8
NBY = 16
CX = 16
CY = 16
CZ = 128
C = 64
SLOTS = 512
MESH = pl.DeviceIdType.MESH
VMEM = pl.BlockSpec(memory_space=pltpu.VMEM)


def halo_kernel(f_ref, lab_ref, perm_ref, p_ref, lx_ref, ly_ref, rows_ref, send_sem, recv_sem):
    bx = lax.axis_index("bx")
    by = lax.axis_index("by")
    xm = lax.rem(bx + NBX - 1, NBX)
    xp = lax.rem(bx + 1, NBX)
    ym = lax.rem(by + NBY - 1, NBY)
    yp = lax.rem(by + 1, NBY)
    around = [(xm, by), (xp, by), (bx, ym), (bx, yp), (xm, ym), (xm, yp), (xp, ym), (xp, yp)]
    barrier = pltpu.get_barrier_semaphore()
    for peer in around:
        pl.semaphore_signal(barrier, inc=1, device_id=peer, device_id_type=MESH)

    rows_ref[...] = lab_ref[:, CY - 1, :]
    perm = perm_ref[...]

    def turned(pair, carry):
        for group in range(C // 16):
            block = jnp.concatenate(
                [
                    f_ref[16 * group : 16 * group + 16, 2 * pair + half].reshape(256, CZ)
                    for half in range(2)
                ],
                axis=1,
            )
            out = jnp.dot(perm, block, preferred_element_type=jnp.float32).astype(jnp.bfloat16)
            for half in range(2):
                p_ref[1 + 2 * pair + half, 1 : CY + 1, 16 * group : 16 * group + 16, :] = out[
                    :, half * CZ : (half + 1) * CZ
                ].reshape(CY, 16, CZ)
        return carry

    lax.fori_loop(0, CX // 2, turned, 0)
    pl.semaphore_wait(barrier, len(around))
    inner = pl.ds(1, CX)
    copies = []

    def send(src, dst, peer):
        at = len(copies)
        copy = pltpu.make_async_remote_copy(
            src_ref=src,
            dst_ref=dst,
            send_sem=send_sem.at[at],
            recv_sem=recv_sem.at[at],
            device_id=peer,
            device_id_type=MESH,
        )
        copy.start()
        copies.append(copy)

    send(p_ref.at[1, inner], p_ref.at[CX + 1, inner], (xm, by))
    send(p_ref.at[CX, inner], p_ref.at[0, inner], (xp, by))
    send(p_ref.at[inner, 1], p_ref.at[inner, CY + 1], (bx, ym))
    send(p_ref.at[inner, CY], p_ref.at[inner, 0], (bx, yp))
    send(p_ref.at[1, 1], p_ref.at[CX + 1, CY + 1], (xm, ym))
    send(p_ref.at[1, CY], p_ref.at[CX + 1, 0], (xm, yp))
    send(p_ref.at[CX, 1], p_ref.at[0, CY + 1], (xp, ym))
    send(p_ref.at[CX, CY], p_ref.at[0, 0], (xp, yp))
    send(lab_ref.at[CX - 1], lx_ref, (xp, by))
    send(rows_ref, ly_ref, (bx, yp))
    for copy in copies:
        copy.wait()

    @pl.when(bx == 0)
    def _():
        p_ref[0] = jnp.zeros((CY + 2, C, CZ), jnp.bfloat16)
        lx_ref[...] = jnp.full((CY, CZ), -1, jnp.int32)

    @pl.when(bx == NBX - 1)
    def _():
        p_ref[CX + 1] = jnp.zeros((CY + 2, C, CZ), jnp.bfloat16)

    @pl.when(by == 0)
    def _():
        p_ref[:, 0] = jnp.zeros((CX + 2, C, CZ), jnp.bfloat16)
        ly_ref[...] = jnp.full((CX, CZ), -1, jnp.int32)

    @pl.when(by == NBY - 1)
    def _():
        p_ref[:, CY + 1] = jnp.zeros((CX + 2, C, CZ), jnp.bfloat16)


def brick_kernel(
    p0_ref,
    p1_ref,
    p2_ref,
    own_ref,
    ox_ref,
    ly_ref,
    w_ref,
    bias_ref,
    head_ref,
    head_bias_ref,
    ends_ref,
    owner_ref,
    row_ref,
    count_ref,
    out_ref,
    logit_ref,
    table_ref,
):
    x = pl.program_id(0)
    lane = lax.broadcasted_iota(jnp.int32, (2 * C, CZ), 1)
    weights = w_ref[...]
    planes = [ref[0].reshape((CY + 2) * C, CZ) for ref in (p0_ref, p1_ref, p2_ref)]
    for t in range(4):
        low = 2 * t * C
        high = low + 8 * C
        stacked = jnp.concatenate(
            [
                jnp.concatenate([plane[low : low + 4 * C], plane[high : high + 4 * C]], axis=1)
                for plane in planes
            ],
            axis=0,
        )
        sums = jnp.dot(weights, stacked, preferred_element_type=jnp.float32)
        halves = []
        for half in range(2):
            part = sums[:, half * CZ : (half + 1) * CZ]
            before = pltpu.roll(part[: 2 * C], 1, 1)
            after = pltpu.roll(part[4 * C :], CZ - 1, 1)
            pre = (
                part[2 * C : 4 * C]
                + jnp.where(lane > 0, before, 0.0)
                + jnp.where(lane < CZ - 1, after, 0.0)
                + bias_ref[...]
            )
            halves.append(jnp.maximum(pre, 0.0).astype(jnp.bfloat16))
        hidden = jnp.concatenate(halves, axis=1)
        logits = jnp.dot(head_ref[...], hidden, preferred_element_type=jnp.float32)
        for d in range(3):
            for half in range(2):
                logit_ref[d, 2 * t + 8 * half : 2 * t + 8 * half + 2, :] = logits[
                    2 * d : 2 * d + 2, half * CZ : (half + 1) * CZ
                ]

    affin = [
        jax.nn.sigmoid(logit_ref[d] + head_bias_ref[d]).astype(jnp.bfloat16).astype(jnp.float32)
        for d in range(3)
    ]
    own_i = own_ref[0]
    line = lax.broadcasted_iota(jnp.int32, (CY, CZ), 0)
    deep = lax.broadcasted_iota(jnp.int32, (CY, CZ), 1)
    edge_line = jnp.broadcast_to(ly_ref[pl.ds(x, 1), :], (CY, CZ))
    own = own_i.astype(jnp.float32)
    oth_x = ox_ref[0].astype(jnp.float32)
    oth_y = jnp.where(line > 0, pltpu.roll(own_i, 1, 0), edge_line).astype(jnp.float32)
    oth_z = jnp.where(deep > 0, pltpu.roll(own_i, 1, 1), -1).astype(jnp.float32)
    same_xy = oth_x == oth_y
    same_xz = oth_x == oth_z
    same_yz = oth_y == oth_z
    sum_x = affin[0] + jnp.where(same_xy, affin[1], 0.0) + jnp.where(same_xz, affin[2], 0.0)
    sum_y = affin[1] + jnp.where(same_yz, affin[2], 0.0)
    top_x = sum_x.astype(jnp.bfloat16).astype(jnp.float32)
    top_y = sum_y.astype(jnp.bfloat16).astype(jnp.float32)
    in_x = same_xy | same_xz
    rest = jnp.where(in_x, sum_x - top_x, sum_y - top_y)
    rest_at = jnp.where(in_x, oth_x, oth_y)

    ids = lax.broadcasted_iota(jnp.int32, (LABELS, CZ), 0).astype(jnp.float32).astype(jnp.bfloat16)

    def spread_row(values, y):
        wide = jnp.broadcast_to(values[y : y + 1, :], (16, CZ)).astype(jnp.bfloat16)
        return jnp.concatenate([wide] * (LABELS // 16), axis=0)

    zero = jnp.zeros((LABELS, CZ), jnp.bfloat16)
    one = jnp.ones((LABELS, CZ), jnp.bfloat16)
    lefts, tops, rests = [], [], []
    for y in range(CY):
        lefts.append(jnp.where(spread_row(own, y) == ids, one, zero))
        tops.append(
            jnp.where(
                spread_row(oth_x, y) == ids,
                spread_row(top_x, y),
                jnp.where(
                    spread_row(oth_y, y) == ids,
                    spread_row(top_y, y),
                    jnp.where(spread_row(oth_z, y) == ids, spread_row(affin[2], y), zero),
                ),
            )
        )
        rests.append(jnp.where(spread_row(rest_at, y) == ids, spread_row(rest, y), zero))
    left = jnp.concatenate(lefts, axis=1)
    right = jnp.concatenate(
        [jnp.concatenate(tops, axis=1), jnp.concatenate(rests, axis=1)], axis=0
    )
    found = lax.dot_general(
        right, left, (((1,), (1,)), ((), ())), preferred_element_type=jnp.float32
    )
    found = found[:LABELS] + found[LABELS:]

    @pl.when(x == 0)
    def _():
        table_ref[...] = found

    @pl.when(x > 0)
    def _():
        table_ref[...] += found

    @pl.when(x == CX - 1)
    def _():
        table = table_ref[...]
        first = ends_ref[0:1, :]
        second = ends_ref[1:2, :]
        label = lax.broadcasted_iota(jnp.int32, (LABELS, SLOTS), 0)
        slot = lax.broadcasted_iota(jnp.int32, (1, SLOTS), 1)
        picked = jnp.dot(
            table + table.T,
            (first == label).astype(jnp.float32),
            precision=lax.Precision.HIGHEST,
            preferred_element_type=jnp.float32,
        )
        value = jnp.sum(jnp.where(second == label, picked, 0.0), axis=0, keepdims=True)
        keep = (slot < count_ref[0]) & (first != second)
        value = jnp.where(keep, value, 0.0)
        owner = owner_ref[...]
        place = (owner % NBY) * NBX + owner // NBY
        row_id = lax.broadcasted_iota(jnp.int32, (EO, SLOTS), 0)
        out_ref[...] = lax.dot_general(
            jnp.where(place == row_id, value, 0.0),
            (row_ref[...] == row_id).astype(jnp.float32),
            (((1,), (1,)), ((), ())),
            precision=lax.Precision.HIGHEST,
            preferred_element_type=jnp.float32,
        )


def gather_kernel(s_ref, o_ref, got_ref, mid_ref, last_ref, send1, recv1, send2, recv2):
    bx = lax.axis_index("bx")
    by = lax.axis_index("by")
    barrier = pltpu.get_barrier_semaphore()
    for step in range(1, NBY):
        peer = (bx, lax.rem(by + step, NBY))
        pl.semaphore_signal(barrier, inc=1, device_id=peer, device_id_type=MESH)
    for step in range(1, NBX):
        peer = (lax.rem(bx + step, NBX), by)
        pl.semaphore_signal(barrier, inc=1, device_id=peer, device_id_type=MESH)
    pl.semaphore_wait(barrier, NBX + NBY - 2)
    copies = []
    for step in range(1, NBY):
        to = lax.rem(by + step, NBY)
        copy = pltpu.make_async_remote_copy(
            src_ref=s_ref.at[to],
            dst_ref=got_ref.at[step],
            send_sem=send1.at[step],
            recv_sem=recv1.at[step],
            device_id=(bx, to),
            device_id_type=MESH,
        )
        copy.start()
        copies.append(copy)
    total = s_ref[by]
    for step in range(1, NBY):
        copies[step - 1].wait()
        total = total + got_ref[step]
    for row in range(NBX):
        mid_ref[row] = total[row : row + 1, :]
    copies = []
    for step in range(1, NBX):
        to = lax.rem(bx + step, NBX)
        copy = pltpu.make_async_remote_copy(
            src_ref=mid_ref.at[to],
            dst_ref=last_ref.at[step],
            send_sem=send2.at[step],
            recv_sem=recv2.at[step],
            device_id=(to, by),
            device_id_type=MESH,
        )
        copy.start()
        copies.append(copy)
    total = mid_ref[bx]
    for step in range(1, NBX):
        copies[step - 1].wait()
        total = total + last_ref[step]
    o_ref[...] = total


def on_device(
    features,
    labels,
    conv_weight,
    conv_bias,
    head_weight,
    head_bias,
    edge_ends,
    edge_owner,
    edge_row,
    edge_count,
):
    spot = jnp.arange(256, dtype=jnp.int32)
    perm = ((spot[:, None] % 16) * 16 + spot[:, None] // 16 == spot[None, :]).astype(jnp.bfloat16)
    padded, plane, edge_line = pl.pallas_call(
        halo_kernel,
        out_shape=(
            jax.ShapeDtypeStruct((CX + 2, CY + 2, C, CZ), jnp.bfloat16),
            jax.ShapeDtypeStruct((CY, CZ), jnp.int32),
            jax.ShapeDtypeStruct((CX, CZ), jnp.int32),
        ),
        in_specs=[VMEM] * 3,
        out_specs=(VMEM,) * 3,
        scratch_shapes=[
            pltpu.VMEM((CX, CZ), jnp.int32),
            pltpu.SemaphoreType.DMA((10,)),
            pltpu.SemaphoreType.DMA((10,)),
        ],
        compiler_params=pltpu.CompilerParams(
            collective_id=0, has_side_effects=True, vmem_limit_bytes=40 * 2**20
        ),
        name="halo",
    )(features, labels, perm)

    taps = conv_weight.reshape(C, 3, 3, 3, C).transpose(3, 0, 1, 2, 4)
    wide = jnp.stack(
        [
            jnp.pad(taps, ((0, 0), (0, 0), (0, 0), (0, 1), (0, 0))),
            jnp.pad(taps, ((0, 0), (0, 0), (0, 0), (1, 0), (0, 0))),
        ],
        axis=1,
    ).reshape(6 * C, 12 * C)
    bias = jnp.broadcast_to(jnp.concatenate([conv_bias, conv_bias])[:, None], (2 * C, CZ))
    blank = jnp.zeros((3, C), jnp.bfloat16)
    head = jnp.stack(
        [
            jnp.concatenate([head_weight, blank], axis=1),
            jnp.concatenate([blank, head_weight], axis=1),
        ],
        axis=1,
    ).reshape(6, 2 * C)
    head = jnp.pad(head, ((0, 10), (0, 0)))
    below_x = jnp.concatenate([plane[None], labels[:-1]], axis=0)

    def whole(*shape):
        return pl.BlockSpec(shape, lambda x: (0,) * len(shape))

    spread = pl.pallas_call(
        brick_kernel,
        grid=(CX,),
        out_shape=jax.ShapeDtypeStruct((EO, EO), jnp.float32),
        in_specs=[
            pl.BlockSpec((1, CY + 2, C, CZ), lambda x: (x, 0, 0, 0)),
            pl.BlockSpec((1, CY + 2, C, CZ), lambda x: (x + 1, 0, 0, 0)),
            pl.BlockSpec((1, CY + 2, C, CZ), lambda x: (x + 2, 0, 0, 0)),
            pl.BlockSpec((1, CY, CZ), lambda x: (x, 0, 0)),
            pl.BlockSpec((1, CY, CZ), lambda x: (x, 0, 0)),
            whole(CX, CZ),
            whole(6 * C, 12 * C),
            whole(2 * C, CZ),
            whole(16, 2 * C),
            pl.BlockSpec(memory_space=pltpu.SMEM),
            whole(2, SLOTS),
            whole(1, SLOTS),
            whole(1, SLOTS),
            pl.BlockSpec(memory_space=pltpu.SMEM),
        ],
        out_specs=whole(EO, EO),
        scratch_shapes=[
            pltpu.VMEM((3, CY, CZ), jnp.float32),
            pltpu.VMEM((LABELS, LABELS), jnp.float32),
        ],
        compiler_params=pltpu.CompilerParams(vmem_limit_bytes=48 * 2**20),
        name="brick",
    )(
        padded,
        padded,
        padded,
        labels,
        below_x,
        edge_line,
        wide,
        bias,
        head,
        head_bias,
        edge_ends[0],
        edge_owner[:, :, 0],
        edge_row,
        edge_count,
    )

    total = pl.pallas_call(
        gather_kernel,
        out_shape=jax.ShapeDtypeStruct((1, EO), jnp.float32),
        in_specs=[VMEM],
        out_specs=VMEM,
        scratch_shapes=[
            pltpu.VMEM((NBY, NBX, EO), jnp.float32),
            pltpu.VMEM((NBX, 1, EO), jnp.float32),
            pltpu.VMEM((NBX, 1, EO), jnp.float32),
            pltpu.SemaphoreType.DMA((NBY,)),
            pltpu.SemaphoreType.DMA((NBY,)),
            pltpu.SemaphoreType.DMA((NBX,)),
            pltpu.SemaphoreType.DMA((NBX,)),
        ],
        compiler_params=pltpu.CompilerParams(collective_id=1, has_side_effects=True),
        name="owners",
    )(spread.reshape(NBY, NBX, EO))
    return total[0]


def solution(mesh):
    placed = (
        P(None, "bx", "by", None),
        P("bx", "by", None),
        P(),
        P(),
        P(),
        P(),
        P(("bx", "by"), None, None),
        P(("bx", "by"), None, None),
        P(("bx", "by"), None),
        P(("bx", "by")),
    )
    return jax.shard_map(
        on_device, mesh=mesh, in_specs=placed, out_specs=P(("bx", "by")), check_vma=False
    )
```

time: 766 us -> 91.5 us (0.12); the launches traced: 757 us -> 91.2 us
  matrix products: 287 us -> 0 us
  local copies, waits for them, and re-layouts: 209 us -> 10.1 us
  waiting for transfers between devices: 150 us -> 0 us
  Pallas kernels: 0 us -> 78.8 us
  other arithmetic: 61 us -> 1.52 us
  loops' own time: 17.7 us -> 0 us
  starting transfers between devices: 17.7 us -> 0 us
  between operations: 14.5 us -> 0.84 us
    dot_general x112 -> x0, matrix products: 287 us -> none  [the longest x104 146 us: one_block(): pre = pre + jnp.dot(weight_tap, piece, preferred_element_type=jnp.float32)]
    unnamed x2 -> x0, waiting for transfers between devices: 142 us -> none
    slice x9 -> x2, local copies, waits for them, and re-layouts: 105 us -> 0.01 us  [on_device(): below_x = jnp.concatenate([plane[None], labels[:-1]], axis=0)]
    while x212 -> x0, local copies, waits for them, and re-layouts: 83.2 us -> none
    pallas_call x0 -> x3, Pallas kernels: none -> 78.8 us  [the longest x1 47.5 us: on_device(): pl.pallas_call(brick_kernel, grid=(CX,), out_shape=jax.ShapeDtypeStruct((...]
    dot_general x4 -> x0, other arithmetic: 44.3 us -> none  [one_block(): lax.dot_general(left, right, (((0,), (0,)), ((), ())), preferred_element_...]
    another operation x1 -> x0, loops' own time: 17.7 us -> none  [brick_sums(): pair_table = jnp.sum(lax.map(one_block, starts), axis=0)]
    ppermute x6 -> x0, starting transfers between devices: 17.7 us -> none  [the longest x2 7.73 us: padded_2(): lax.ppermute(tail, axis, [(i, (i + 1) % count) for i in range(ends)])]
  transfers between devices with their start and end apart: 7 -> 0, of which waited for: 3 -> 0; matrix products, arithmetic and copies ran while one was open for 1% -> 0% of each run, Pallas kernels for 0% -> 0%
where the time goes in v1:
time: 91.5 us; the launch traced here: 91.2 us
  Pallas kernels  78.8 us (86%)
  local copies, waits for them, and re-layouts  10.1 us (11%)
  other arithmetic  1.52 us (2%)
    pallas_call x1, Pallas kernels, on_device(): pl.pallas_call(brick_kernel, grid=(CX,), out_shape=jax.ShapeDtypeStruct((...  47.5 us
    pallas_call x1, Pallas kernels, on_device(): pl.pallas_call(halo_kernel, out_shape=(jax.ShapeDtypeStruct((CX + 2, CY +...  17.8 us
    pallas_call x1, Pallas kernels, on_device(): pl.pallas_call(gather_kernel, out_shape=jax.ShapeDtypeStruct((1, EO), jnp...  13.5 us
    unnamed x21, local copies, waits for them, and re-layouts  6.43 us

profile of v1, /device:TPU:1, one launch (start us, length us, event | category | flops | bytes accessed | tf_op | source)
XLA Modules:
  0.0 91.2 jit_solution(6737248558450538969)
XLA Ops:
  0.0 1.5 %reshape.68 = bf16[64,3,3,3,64]{4,3,2,1,0:T(4,128)(2,1)S(1)} reshape(bf16[64,1728]{1,0:T(8,128)(2,1)} %param.12) | data formatting | bytes 442368 | tf_op jit(solution)/shard_map/reshape | solution.py:333
  1.5 0.7 pad_bitcast_fusion.1
  2.3 1.3 %pad_maximum_fusion = bf16[3,2,64,3,4,64]{5,0,4,3,2,1:T(4,128)(2,1)S(1)} fusion(bf16[3,1,64,3,4,64]{5,0,4,3,2,1:T(4,128)(2,1)S(1)} %get-tuple-element.12, bf16[3,1,64,3,4,64]{5,0,4,3,2,1:T(4,128)(2,1)S(1)} %get-tuple-element.11), kind=kLoop, calls=%fused_computation | loop fusion | flops 294912 | bytes 1179648 | tf_op jit(solution)/shard_map/stack | solution.py:334
  3.6 0.5 copy.14
  4.1 0.0 copy-start.2
  4.1 0.7 reshape.69.w_ref
  4.8 0.1 fusion.perm_ref
  4.9 0.1 copy-done.2
  5.0 0.0 copy-start.1
  5.0 2.2 %copy-done.1 = bf16[64,16,16,128]{3,2,1,0:T(8,128)(2,1)S(1)} copy-done((bf16[64,16,16,128]{3,2,1,0:T(8,128)(2,1)S(1)}, bf16[64,16,16,128]{3,2,1,0:T(8,128)(2,1)}, u32[]{:S(2)}) %copy-start.1) | copy-done | bytes 4194328
  7.2 0.0 slice-start
  7.2 0.0 copy-start.8
  7.2 0.0 copy-start.9
  7.2 0.0 copy-start.4
  7.2 0.0 copy-start.5
  7.2 0.0 copy-start.6
  7.2 0.0 copy-start.7
  7.2 17.8 %halo.1 = (bf16[18,18,64,128]{3,2,1,0:T(8,128)(2,1)S(1)}, s32[16,128]{1,0:T(8,128)S(1)}, s32[16,128]{1,0:T(8,128)S(1)}) custom-call(bf16[64,16,16,128]{3,2,1,0:T(8,128)(2,1)S(1)} %copy-done.1, s32[16,16,128]{2,1,0:T(8,128)S(1)} %copy-done.2, bf16[256,256]{1,0:T(8,128)(2,1)S(1)} %fusion.perm_ref), custom_call_target="tpu_custom_call" | custom-call | tf_op jit(solution)/shard_map/halo/pallas_call | solution.py:313
  25.1 0.0 copy-start
  25.1 2.3 %copy-done = bf16[18,18,64,128]{3,2,1,0:T(8,128)(2,1)} copy-done((bf16[18,18,64,128]{3,2,1,0:T(8,128)(2,1)}, bf16[18,18,64,128]{3,2,1,0:T(8,128)(2,1)S(1)}, u32[]{:S(2)}) %copy-start) | copy-done | bytes 5308440
  27.4 0.0 slice-done
  27.4 0.0 copy-done.8
  27.4 0.1 pad_bitcast_fusion.3
  27.6 0.0 copy-done.9
  27.6 0.1 pad_maximum_fusion.2
  27.6 0.1 broadcast_in_dim.5.bias_ref
  28.4 0.0 copy-done.4
  28.4 0.0 copy-done.5
  28.4 0.0 copy-done.6
  28.4 0.0 copy-done.7
  28.4 47.5 %brick.1 = f32[128,128]{1,0:T(8,128)S(1)} custom-call(bf16[18,18,64,128]{3,2,1,0:T(8,128)(2,1)} %copy-done, bf16[18,18,64,128]{3,2,1,0:T(8,128)(2,1)} %copy-done, bf16[18,18,64,128]{3,2,1,0:T(8,128)(2,1)} %copy-done, s32[16,16,128]{2,1,0:T(8,128)S(1)} %copy-done.2, s32[16,16,128]{2,1,0:T(8,128)S(1)} %pad_add_fusion.ox_ref, ...), custom_call_target="tpu_custom_call" | custom-call | tf_op jit(solution)/shard_map/brick/pallas_call | solution.py:356
  75.9 0.0 copy-start.3
  75.9 0.6 copy-done.3
  76.5 13.5 %owners.1 = f32[1,128]{1,0:T(1,128)} custom-call(f32[16,8,128]{2,1,0:T(8,128)} %bitcast.14), custom_call_target="tpu_custom_call" | custom-call | tf_op jit(solution)/shard_map/owners/pallas_call | solution.py:400
  90.0 1.2 %copy.18 = f32[128]{0:T(128)} copy(f32[128]{0:T(128)} %bitcast.19) | data formatting | bytes 1024
  (6 shorter events, 0.1 us)
Async XLA Ops:
  4.1 0.9 copy-start.2
  5.0 2.2 %copy-start.1 = (bf16[64,16,16,128]{3,2,1,0:T(8,128)(2,1)S(1)}, bf16[64,16,16,128]{3,2,1,0:T(8,128)(2,1)}, u32[]{:S(2)}) copy-start(bf16[64,16,16,128]{3,2,1,0:T(8,128)(2,1)} %f_ref.1) | copy-start | bytes 12582916
  7.2 20.2 %slice-start = ((s32[16,16,128]{2,1,0:T(8,128)}), s32[15,16,128]{2,1,0:T(8,128)S(1)}, s32[]{:S(2)}) async-start(s32[16,16,128]{2,1,0:T(8,128)} %own_ref.1), calls=%async_computation | async-start | bytes 245760 | tf_op jit(solution)/shard_map/slice | solution.py:351
  7.2 20.2 %copy-start.8 = (bf16[3,64]{1,0:T(4,128)(2,1)S(1)}, bf16[3,64]{1,0:T(4,128)(2,1)}, u32[]{:S(2)}) copy-start(bf16[3,64]{1,0:T(4,128)(2,1)} %param.14) | copy-start | bytes 1156
  7.2 20.4 %copy-start.9 = (f32[64]{0:T(128)S(1)}, f32[64]{0:T(128)}, u32[]{:S(2)}) copy-start(f32[64]{0:T(128)} %param.13) | copy-start | bytes 772
  7.2 21.2 %copy-start.4 = (s32[1,2,512]{2,1,0:T(2,128)S(1)}, s32[1,2,512]{2,1,0:T(2,128)}, u32[]{:S(2)}) copy-start(s32[1,2,512]{2,1,0:T(2,128)} %param.16) | copy-start | bytes 12292
  7.2 21.2 %copy-start.5 = (s32[1,512,1]{1,2,0:T(1,128)S(1)}, s32[1,512,1]{1,2,0:T(1,128)}, u32[]{:S(2)}) copy-start(s32[1,512,1]{1,2,0:T(1,128)} %param.17) | copy-start | bytes 6148
  7.2 21.2 %copy-start.6 = (s32[1,512]{1,0:T(1,128)S(1)}, s32[1,512]{1,0:T(1,128)}, u32[]{:S(2)}) copy-start(s32[1,512]{1,0:T(1,128)} %row_ref.1) | copy-start | bytes 6148
  7.2 21.2 %copy-start.7 = (f32[3]{0:T(128)S(1)}, f32[3]{0:T(128)}, u32[]{:S(2)}) copy-start(f32[3]{0:T(128)} %head_bias_ref.1) | copy-start | bytes 40
  25.1 2.3 %copy-start = (bf16[18,18,64,128]{3,2,1,0:T(8,128)(2,1)}, bf16[18,18,64,128]{3,2,1,0:T(8,128)(2,1)S(1)}, u32[]{:S(2)}) copy-start(bf16[18,18,64,128]{3,2,1,0:T(8,128)(2,1)S(1)} %get-tuple-element.8.p0_ref.p1_ref.p2_ref) | copy-start | bytes 15925252
  75.9 0.6 copy-start.3

commit v2 on v0

v2 whole, which is shorter than its diff:
```python
import jax
import jax.numpy as jnp
from jax import lax
from jax.experimental import pallas as pl
from jax.experimental.pallas import tpu as pltpu
from jax.sharding import PartitionSpec as P

LABELS = 256
EO = 128
NBX = 8
NBY = 16
CX = 16
CY = 16
CZ = 128
C = 64
SLOTS = 512
PAIRS = CY // 2
MESH = pl.DeviceIdType.MESH
VMEM = pl.BlockSpec(memory_space=pltpu.VMEM)
SMEM = pl.BlockSpec(memory_space=pltpu.SMEM)


def lay_weights(conv_ref, w_ref):
    blank = jnp.zeros((C, C), jnp.bfloat16)
    for dz in range(3):
        for out_y in range(2):
            pieces = []
            for dx in range(3):
                for in_y in range(4):
                    dy = in_y - out_y
                    at = (9 * dx + 3 * dy + dz) * C
                    pieces.append(conv_ref[:, at : at + C] if 0 <= dy <= 2 else blank)
            w_ref[(2 * dz + out_y) * C : (2 * dz + out_y + 1) * C, :] = jnp.concatenate(
                pieces, axis=1
            )


def conv_plane(x, p_ref, w_ref, bias_ref, head_ref, head_bias_ref, logit_ref):
    lane = lax.broadcasted_iota(jnp.int32, (2 * C, CZ), 1)
    stacked = jnp.concatenate(
        [
            jnp.concatenate(
                [p_ref[x + dx, 2 * j : 2 * j + 4].reshape(4 * C, CZ) for j in range(PAIRS)], axis=1
            )
            for dx in range(3)
        ],
        axis=0,
    )
    sums = jnp.dot(w_ref[...], stacked, preferred_element_type=jnp.float32)
    parts = []
    for j in range(PAIRS):
        part = sums[:, j * CZ : (j + 1) * CZ]
        before = pltpu.roll(part[: 2 * C], 1, 1)
        after = pltpu.roll(part[4 * C :], CZ - 1, 1)
        pre = (
            part[2 * C : 4 * C]
            + jnp.where(lane > 0, before, 0.0)
            + jnp.where(lane < CZ - 1, after, 0.0)
            + bias_ref[...]
        )
        parts.append(jnp.maximum(pre, 0.0).astype(jnp.bfloat16))
    hidden = jnp.concatenate(parts, axis=1)
    logits = jnp.dot(head_ref[...], hidden, preferred_element_type=jnp.float32)
    for d in range(3):
        for j in range(PAIRS):
            logit_ref[d, 2 * j : 2 * j + 2, :] = (
                logits[2 * d : 2 * d + 2, j * CZ : (j + 1) * CZ] + head_bias_ref[d]
            )


def pair_sums(x, logit_ref, lab_ref, line_ref):
    affin = [
        jax.nn.sigmoid(logit_ref[d]).astype(jnp.bfloat16).astype(jnp.float32) for d in range(3)
    ]
    own_i = lab_ref[x + 1]
    line = lax.broadcasted_iota(jnp.int32, (CY, CZ), 0)
    deep = lax.broadcasted_iota(jnp.int32, (CY, CZ), 1)
    edge_line = jnp.broadcast_to(line_ref[pl.ds(x, 1), :], (CY, CZ))
    own = own_i.astype(jnp.float32)
    oth_x = lab_ref[x].astype(jnp.float32)
    oth_y = jnp.where(line > 0, pltpu.roll(own_i, 1, 0), edge_line).astype(jnp.float32)
    oth_z = jnp.where(deep > 0, pltpu.roll(own_i, 1, 1), -1).astype(jnp.float32)
    same_xy = oth_x == oth_y
    same_xz = oth_x == oth_z
    same_yz = oth_y == oth_z
    sum_x = affin[0] + jnp.where(same_xy, affin[1], 0.0) + jnp.where(same_xz, affin[2], 0.0)
    sum_y = affin[1] + jnp.where(same_yz, affin[2], 0.0)
    top_x = sum_x.astype(jnp.bfloat16).astype(jnp.float32)
    top_y = sum_y.astype(jnp.bfloat16).astype(jnp.float32)
    in_x = same_xy | same_xz
    rest = jnp.where(in_x, sum_x - top_x, sum_y - top_y)
    rest_at = jnp.where(in_x, oth_x, oth_y)

    ids = lax.broadcasted_iota(jnp.int32, (LABELS, CZ), 0).astype(jnp.float32).astype(jnp.bfloat16)

    def spread_row(values, y):
        wide = jnp.broadcast_to(values[y : y + 1, :], (16, CZ)).astype(jnp.bfloat16)
        return jnp.concatenate([wide] * (LABELS // 16), axis=0)

    zero = jnp.zeros((LABELS, CZ), jnp.bfloat16)
    one = jnp.ones((LABELS, CZ), jnp.bfloat16)
    lefts, tops, rests = [], [], []
    for y in range(CY):
        lefts.append(jnp.where(spread_row(own, y) == ids, one, zero))
        tops.append(
            jnp.where(
                spread_row(oth_x, y) == ids,
                spread_row(top_x, y),
                jnp.where(
                    spread_row(oth_y, y) == ids,
                    spread_row(top_y, y),
                    jnp.where(spread_row(oth_z, y) == ids, spread_row(affin[2], y), zero),
                ),
            )
        )
        rests.append(jnp.where(spread_row(rest_at, y) == ids, spread_row(rest, y), zero))
    left = jnp.concatenate(lefts, axis=1)
    right = jnp.concatenate(
        [jnp.concatenate(tops, axis=1), jnp.concatenate(rests, axis=1)], axis=0
    )
    found = lax.dot_general(
        right, left, (((1,), (1,)), ((), ())), preferred_element_type=jnp.float32
    )
    return found[:LABELS] + found[LABELS:]


def slot_rows(table, ends_ref, owner_ref, row_ref, count_ref):
    first = ends_ref[0:1, :]
    second = ends_ref[1:2, :]
    label = lax.broadcasted_iota(jnp.int32, (LABELS, SLOTS), 0)
    slot = lax.broadcasted_iota(jnp.int32, (1, SLOTS), 1)
    picked = jnp.dot(
        table + table.T,
        (first == label).astype(jnp.float32),
        precision=lax.Precision.HIGHEST,
        preferred_element_type=jnp.float32,
    )
    value = jnp.sum(jnp.where(second == label, picked, 0.0), axis=0, keepdims=True)
    keep = (slot < count_ref[0]) & (first != second)
    value = jnp.where(keep, value, 0.0)
    owner = owner_ref[...]
    place = (owner & (NBY - 1)) * NBX + (owner >> 4)
    row_id = lax.broadcasted_iota(jnp.int32, (EO, SLOTS), 0)
    return lax.dot_general(
        jnp.where(place == row_id, value, 0.0),
        (row_ref[...] == row_id).astype(jnp.float32),
        (((1,), (1,)), ((), ())),
        precision=lax.Precision.HIGHEST,
        preferred_element_type=jnp.float32,
    )


def whole_kernel(
    f_ref,
    own_ref,
    conv_ref,
    bias_ref,
    head_ref,
    head_bias_ref,
    ends_ref,
    owner_ref,
    row_ref,
    count_ref,
    o_ref,
    fbuf_ref,
    p_ref,
    lab_ref,
    line_ref,
    last_line_ref,
    w_ref,
    logit_ref,
    table_ref,
    rows_ref,
    got_ref,
    mid_ref,
    last_ref,
    load_sem,
    y_send,
    y_recv,
    x_send,
    x_recv,
    send1,
    recv1,
    send2,
    recv2,
):
    bx = lax.axis_index("bx")
    by = lax.axis_index("by")
    xm = lax.rem(bx + NBX - 1, NBX)
    xp = lax.rem(bx + 1, NBX)
    ym = lax.rem(by + NBY - 1, NBY)
    yp = lax.rem(by + 1, NBY)
    barrier = pltpu.get_barrier_semaphore()

    def greet(peer):
        pl.semaphore_signal(barrier, inc=1, device_id=peer, device_id_type=MESH)

    for step in range(1, NBY):
        greet((bx, lax.rem(by + step, NBY)))
    for step in range(1, NBX):
        greet((lax.rem(bx + step, NBX), by))
    for peer in ((xm, ym), (xm, yp), (xp, ym), (xp, yp)):
        greet(peer)

    def load(pair):
        at = pl.ds(2 * pair, 2)
        return pltpu.make_async_copy(f_ref.at[:, at], fbuf_ref.at[:, at], load_sem.at[pair])

    for pair in range(CX // 2):
        load(pair).start()

    lab_ref[1:] = own_ref[...]
    last_line_ref[...] = own_ref[:, CY - 1, :]
    table_ref[...] = jnp.zeros((LABELS, LABELS), jnp.float32)
    lay_weights(conv_ref, w_ref)
    to = lax.broadcasted_iota(jnp.int32, (256, 256), 0)
    come = lax.broadcasted_iota(jnp.int32, (256, 256), 1)
    perm = ((to & 15) * 16 + (to >> 4) == come).astype(jnp.float32).astype(jnp.bfloat16)
    pl.semaphore_wait(barrier, NBX + NBY + 2)

    def remote(src, dst, send_sem, recv_sem, peer):
        return pltpu.make_async_remote_copy(
            src_ref=src,
            dst_ref=dst,
            send_sem=send_sem,
            recv_sem=recv_sem,
            device_id=peer,
            device_id_type=MESH,
        )

    def y_copies(pair):
        at = pl.ds(1 + 2 * pair, 2)
        return (
            remote(
                p_ref.at[at, 1], p_ref.at[at, CY + 1], y_send.at[0, pair], y_recv.at[0, pair], (bx, ym)
            ),
            remote(
                p_ref.at[at, CY], p_ref.at[at, 0], y_send.at[1, pair], y_recv.at[1, pair], (bx, yp)
            ),
        )

    inner = pl.ds(1, CY)
    x_copies = [
        remote(src, dst, x_send.at[n], x_recv.at[n], peer)
        for n, (src, dst, peer) in enumerate(
            [
                (p_ref.at[1, inner], p_ref.at[CX + 1, inner], (xm, by)),
                (p_ref.at[1, 1], p_ref.at[CX + 1, CY + 1], (xm, ym)),
                (p_ref.at[1, CY], p_ref.at[CX + 1, 0], (xm, yp)),
                (p_ref.at[CX, inner], p_ref.at[0, inner], (xp, by)),
                (p_ref.at[CX, 1], p_ref.at[0, CY + 1], (xp, ym)),
                (p_ref.at[CX, CY], p_ref.at[0, 0], (xp, yp)),
                (own_ref.at[CX - 1], lab_ref.at[0], (xp, by)),
                (last_line_ref, line_ref, (bx, yp)),
            ]
        )
    ]

    def turned(n, carry):
        pair = lax.rem(n + CX // 2 - 1, CX // 2)
        load(pair).wait()
        for group in range(C // 16):
            block = jnp.concatenate(
                [
                    fbuf_ref[16 * group : 16 * group + 16, 2 * pair + half].reshape(256, CZ)
                    for half in range(2)
                ],
                axis=1,
            )
            out = jnp.dot(perm, block, preferred_element_type=jnp.float32).astype(jnp.bfloat16)
            for half in range(2):
                p_ref[1 + 2 * pair + half, 1 : CY + 1, 16 * group : 16 * group + 16, :] = out[
                    :, half * CZ : (half + 1) * CZ
                ].reshape(CY, 16, CZ)
        for copy in y_copies(pair):
            copy.start()
        return carry

    lax.fori_loop(0, 2, turned, 0)
    for copy in x_copies:
        copy.start()
    lax.fori_loop(2, CX // 2, turned, 0)
    for copy in x_copies:
        copy.wait()
    for pair in range(CX // 2):
        for copy in y_copies(pair):
            copy.wait()

    @pl.when(bx == 0)
    def _():
        p_ref[0] = jnp.zeros((CY + 2, C, CZ), jnp.bfloat16)
        lab_ref[0] = jnp.full((CY, CZ), -1, jnp.int32)

    @pl.when(bx == NBX - 1)
    def _():
        p_ref[CX + 1] = jnp.zeros((CY + 2, C, CZ), jnp.bfloat16)

    @pl.when(by == 0)
    def _():
        p_ref[:, 0] = jnp.zeros((CX + 2, C, CZ), jnp.bfloat16)
        line_ref[...] = jnp.full((CX, CZ), -1, jnp.int32)

    @pl.when(by == NBY - 1)
    def _():
        p_ref[:, CY + 1] = jnp.zeros((CX + 2, C, CZ), jnp.bfloat16)

    conv_plane(0, p_ref, w_ref, bias_ref, head_ref, head_bias_ref, logit_ref)

    def plane(x, carry):
        found = pair_sums(x - 1, logit_ref, lab_ref, line_ref)
        conv_plane(x, p_ref, w_ref, bias_ref, head_ref, head_bias_ref, logit_ref)
        table_ref[...] += found
        return carry

    lax.fori_loop(1, CX, plane, 0)
    table = table_ref[...] + pair_sums(CX - 1, logit_ref, lab_ref, line_ref)
    rows_ref[...] = slot_rows(table, ends_ref, owner_ref, row_ref, count_ref).reshape(NBY, NBX, EO)

    copies = []
    for step in range(1, NBY):
        to = lax.rem(by + step, NBY)
        copies.append(
            remote(rows_ref.at[to], got_ref.at[step], send1.at[step], recv1.at[step], (bx, to))
        )
        copies[-1].start()
    total = rows_ref[by]
    for step in range(1, NBY):
        copies[step - 1].wait()
        total = total + got_ref[step]
    for row in range(NBX):
        mid_ref[row] = total[row : row + 1, :]
    copies = []
    for step in range(1, NBX):
        to = lax.rem(bx + step, NBX)
        copies.append(
            remote(mid_ref.at[to], last_ref.at[step], send2.at[step], recv2.at[step], (to, by))
        )
        copies[-1].start()
    total = mid_ref[bx]
    for step in range(1, NBX):
        copies[step - 1].wait()
        total = total + last_ref[step]
    o_ref[...] = total


def on_device(
    features,
    labels,
    conv_weight,
    conv_bias,
    head_weight,
    head_bias,
    edge_ends,
    edge_owner,
    edge_row,
    edge_count,
):
    bias = jnp.broadcast_to(jnp.concatenate([conv_bias, conv_bias])[:, None], (2 * C, CZ))
    blank = jnp.zeros((3, C), jnp.bfloat16)
    head = jnp.stack(
        [
            jnp.concatenate([head_weight, blank], axis=1),
            jnp.concatenate([blank, head_weight], axis=1),
        ],
        axis=1,
    ).reshape(6, 2 * C)
    head = jnp.pad(head, ((0, 10), (0, 0)))
    bf16, f32, i32 = jnp.bfloat16, jnp.float32, jnp.int32
    total = pl.pallas_call(
        whole_kernel,
        out_shape=jax.ShapeDtypeStruct((1, EO), f32),
        in_specs=[pl.BlockSpec(memory_space=pl.ANY)] + [VMEM] * 4 + [SMEM] + [VMEM] * 3 + [SMEM],
        out_specs=VMEM,
        scratch_shapes=[
            pltpu.VMEM((C, CX, CY, CZ), bf16),
            pltpu.VMEM((CX + 2, CY + 2, C, CZ), bf16),
            pltpu.VMEM((CX + 1, CY, CZ), i32),
            pltpu.VMEM((CX, CZ), i32),
            pltpu.VMEM((CX, CZ), i32),
            pltpu.VMEM((6 * C, 12 * C), bf16),
            pltpu.VMEM((3, CY, CZ), f32),
            pltpu.VMEM((LABELS, LABELS), f32),
            pltpu.VMEM((NBY, NBX, EO), f32),
            pltpu.VMEM((NBY, NBX, EO), f32),
            pltpu.VMEM((NBX, 1, EO), f32),
            pltpu.VMEM((NBX, 1, EO), f32),
            pltpu.SemaphoreType.DMA((CX // 2,)),
            pltpu.SemaphoreType.DMA((2, CX // 2)),
            pltpu.SemaphoreType.DMA((2, CX // 2)),
            pltpu.SemaphoreType.DMA((8,)),
            pltpu.SemaphoreType.DMA((8,)),
            pltpu.SemaphoreType.DMA((NBY,)),
            pltpu.SemaphoreType.DMA((NBY,)),
            pltpu.SemaphoreType.DMA((NBX,)),
            pltpu.SemaphoreType.DMA((NBX,)),
        ],
        compiler_params=pltpu.CompilerParams(
            collective_id=0, has_side_effects=True, vmem_limit_bytes=52 * 2**20
        ),
        name="whole",
    )(
        features,
        labels,
        conv_weight,
        bias,
        head,
        head_bias,
        edge_ends[0],
        edge_owner[:, :, 0],
        edge_row,
        edge_count,
    )
    return total[0]


def solution(mesh):
    placed = (
        P(None, "bx", "by", None),
        P("bx", "by", None),
        P(),
        P(),
        P(),
        P(),
        P(("bx", "by"), None, None),
        P(("bx", "by"), None, None),
        P(("bx", "by"), None),
        P(("bx", "by")),
    )
    return jax.shard_map(
        on_device, mesh=mesh, in_specs=placed, out_specs=P(("bx", "by")), check_vma=False
    )
```

time: 766 us -> 64.2 us (0.08); the launches traced: 757 us -> 63.9 us
  matrix products: 287 us -> 0 us
  local copies, waits for them, and re-layouts: 209 us -> 6 us
  waiting for transfers between devices: 150 us -> 0 us
  other arithmetic: 61 us -> 0.82 us
  Pallas kernels: 0 us -> 56.4 us
  loops' own time: 17.7 us -> 0 us
  starting transfers between devices: 17.7 us -> 0 us
  between operations: 14.5 us -> 0.68 us
    dot_general x112 -> x0, matrix products: 287 us -> none  [the longest x104 146 us: one_block(): pre = pre + jnp.dot(weight_tap, piece, preferred_element_type=jnp.float32)]
    unnamed x2 -> x0, waiting for transfers between devices: 142 us -> none
    slice x9 -> x0, local copies, waits for them, and re-layouts: 105 us -> none  [the longest x4 104 us: one_block(): block[:, dx:dx + stride, dy:dy + rows, dz:dz + depth].reshape(chans, width)]
    while x212 -> x0, local copies, waits for them, and re-layouts: 83.2 us -> none
    pallas_call x0 -> x1, Pallas kernels: none -> 56.4 us  [on_device(): pl.pallas_call(whole_kernel, out_shape=jax.ShapeDtypeStruct((1, EO), f32)...]
    dot_general x4 -> x0, other arithmetic: 44.3 us -> none  [one_block(): lax.dot_general(left, right, (((0,), (0,)), ((), ())), preferred_element_...]
    another operation x1 -> x0, loops' own time: 17.7 us -> none  [brick_sums(): pair_table = jnp.sum(lax.map(one_block, starts), axis=0)]
    ppermute x6 -> x0, starting transfers between devices: 17.7 us -> none  [the longest x2 7.73 us: padded_2(): lax.ppermute(tail, axis, [(i, (i + 1) % count) for i in range(ends)])]
  transfers between devices with their start and end apart: 7 -> 0, of which waited for: 3 -> 0; matrix products, arithmetic and copies ran while one was open for 1% -> 0% of each run, Pallas kernels for 0% -> 0%
where the time goes in v2:
time: 64.2 us; the launch traced here: 63.9 us
  Pallas kernels  56.4 us (88%)
  local copies, waits for them, and re-layouts  6 us (9%)
  other arithmetic  0.82 us (1%)
  between operations  0.68 us (1%)
    pallas_call x1, Pallas kernels, on_device(): pl.pallas_call(whole_kernel, out_shape=jax.ShapeDtypeStruct((1, EO), f32)...  56.4 us
    unnamed x13, local copies, waits for them, and re-layouts  5.06 us

profile of v2, /device:TPU:1, one launch (start us, length us, event | category | flops | bytes accessed | tf_op | source)
XLA Modules:
  0.0 63.9 jit_solution(10823921886325228026)
XLA Ops:
  0.7 0.8 %pad_maximum_fusion.1 = f32[128]{0:T(128)S(1)} fusion(f32[64]{0:T(128)} %param.13), kind=kLoop, calls=%fused_computation.3 | loop fusion | flops 128 | bytes 768 | tf_op jit(solution)/shard_map/concatenate | solution.py:358
  1.5 0.8 %pad_bitcast_fusion.1 = (bf16[3,1,128]{2,0,1:T(4,128)(2,1)S(1)}, bf16[3,1,128]{2,0,1:T(4,128)(2,1)S(1)}) fusion(bf16[3,64]{1,0:T(4,128)(2,1)} %param.14), kind=kLoop, calls=%fused_computation.2 | loop fusion | bytes 1920 | tf_op jit(solution)/shard_map/stack | solution.py:360
  2.3 0.1 broadcast_in_dim.2.bias_ref
  2.4 0.0 copy-start
  2.4 0.9 %copy-done = bf16[64,1728]{1,0:T(8,128)(2,1)S(1)} copy-done((bf16[64,1728]{1,0:T(8,128)(2,1)S(1)}, bf16[64,1728]{1,0:T(8,128)(2,1)}, u32[]{:S(2)}) %copy-start) | copy-done | bytes 221208
  3.4 0.0 copy-start.1
  3.4 0.9 %copy-done.1 = s32[16,16,128]{2,1,0:T(8,128)S(1)} copy-done((s32[16,16,128]{2,1,0:T(8,128)S(1)}, s32[16,16,128]{2,1,0:T(8,128)}, u32[]{:S(2)}) %copy-start.1) | copy-done | bytes 131096
  4.3 0.0 copy-start.2
  4.3 0.7 %copy-done.2 = s32[1,2,512]{2,1,0:T(2,128)S(1)} copy-done((s32[1,2,512]{2,1,0:T(2,128)S(1)}, s32[1,2,512]{2,1,0:T(2,128)}, u32[]{:S(2)}) %copy-start.2) | copy-done | bytes 4120
  4.9 0.0 copy-start.3
  5.0 0.7 %copy-done.3 = s32[1,512,1]{1,2,0:T(1,128)S(1)} copy-done((s32[1,512,1]{1,2,0:T(1,128)S(1)}, s32[1,512,1]{1,2,0:T(1,128)}, u32[]{:S(2)}) %copy-start.3) | copy-done | bytes 2072
  5.6 0.0 copy-start.4
  5.6 0.7 %copy-done.4 = s32[1,512]{1,0:T(1,128)S(1)} copy-done((s32[1,512]{1,0:T(1,128)S(1)}, s32[1,512]{1,0:T(1,128)}, u32[]{:S(2)}) %copy-start.4) | copy-done | bytes 2072
  6.3 0.0 copy-start.5
  6.3 0.7 %copy-done.5 = f32[3]{0:T(128)S(1)} copy-done((f32[3]{0:T(128)S(1)}, f32[3]{0:T(128)}, u32[]{:S(2)}) %copy-start.5) | copy-done | bytes 36
  7.0 56.4 %whole.1 = f32[1,128]{1,0:T(1,128)S(1)} custom-call(bf16[64,16,16,128]{3,2,1,0:T(8,128)(2,1)} %f_ref.1, s32[16,16,128]{2,1,0:T(8,128)S(1)} %copy-done.1, bf16[64,1728]{1,0:T(8,128)(2,1)S(1)} %copy-done, f32[128,128]{1,0:T(8,128)S(1)} %broadcast_in_dim.2.bias_ref, bf16[16,128]{1,0:T(8,128)(2,1)S(1)} %pad.6.head_ref, f32[3]{0:T(128)S(1)} %copy-done.5, ...), custom_call_target="tpu_custom_call" | custom-call | tf_op jit(solution)/shard_map/whole/pallas_call | solution.py:369
  63.4 0.5 copy.14
  (4 shorter events, 0.0 us)
Async XLA Ops:
  2.4 0.9 %copy-start = (bf16[64,1728]{1,0:T(8,128)(2,1)S(1)}, bf16[64,1728]{1,0:T(8,128)(2,1)}, u32[]{:S(2)}) copy-start(bf16[64,1728]{1,0:T(8,128)(2,1)} %conv_ref.1) | copy-start | bytes 663556
  3.4 0.9 %copy-start.1 = (s32[16,16,128]{2,1,0:T(8,128)S(1)}, s32[16,16,128]{2,1,0:T(8,128)}, u32[]{:S(2)}) copy-start(s32[16,16,128]{2,1,0:T(8,128)} %own_ref.1) | copy-start | bytes 393220
  4.3 0.7 %copy-start.2 = (s32[1,2,512]{2,1,0:T(2,128)S(1)}, s32[1,2,512]{2,1,0:T(2,128)}, u32[]{:S(2)}) copy-start(s32[1,2,512]{2,1,0:T(2,128)} %param.16) | copy-start | bytes 12292
  4.9 0.7 %copy-start.3 = (s32[1,512,1]{1,2,0:T(1,128)S(1)}, s32[1,512,1]{1,2,0:T(1,128)}, u32[]{:S(2)}) copy-start(s32[1,512,1]{1,2,0:T(1,128)} %param.17) | copy-start | bytes 6148
  5.6 0.7 %copy-start.4 = (s32[1,512]{1,0:T(1,128)S(1)}, s32[1,512]{1,0:T(1,128)}, u32[]{:S(2)}) copy-start(s32[1,512]{1,0:T(1,128)} %row_ref.1) | copy-start | bytes 6148
  6.3 0.7 %copy-start.5 = (f32[3]{0:T(128)S(1)}, f32[3]{0:T(128)}, u32[]{:S(2)}) copy-start(f32[3]{0:T(128)} %head_bias_ref.1) | copy-start | bytes 40

commit v3 on v2

--- a/solution.py
+++ b/solution.py
@@ -17,7 +17,6 @@
 PAIRS = CY // 2
 MESH = pl.DeviceIdType.MESH
 VMEM = pl.BlockSpec(memory_space=pltpu.VMEM)
-SMEM = pl.BlockSpec(memory_space=pltpu.SMEM)
 
 
 def lay_weights(conv_ref, w_ref):
@@ -59,12 +58,13 @@
             + bias_ref[...]
         )
         parts.append(jnp.maximum(pre, 0.0).astype(jnp.bfloat16))
-    hidden = jnp.concatenate(parts, axis=1)
+    hidden = jnp.concatenate([part[:C] for part in parts] + [part[C:] for part in parts], axis=1)
     logits = jnp.dot(head_ref[...], hidden, preferred_element_type=jnp.float32)
     for d in range(3):
-        for j in range(PAIRS):
-            logit_ref[d, 2 * j : 2 * j + 2, :] = (
-                logits[2 * d : 2 * d + 2, j * CZ : (j + 1) * CZ] + head_bias_ref[d]
+        for y in range(CY):
+            at = (y % 2) * PAIRS + y // 2
+            logit_ref[d, y : y + 1, :] = (
+                logits[d : d + 1, at * CZ : (at + 1) * CZ] + head_bias_ref[d]
             )
 
 
@@ -125,8 +125,8 @@
 
 
 def slot_rows(table, ends_ref, owner_ref, row_ref, count_ref):
-    first = ends_ref[0:1, :]
-    second = ends_ref[1:2, :]
+    first = ends_ref[0, 0:1, :]
+    second = ends_ref[0, 1:2, :]
     label = lax.broadcasted_iota(jnp.int32, (LABELS, SLOTS), 0)
     slot = lax.broadcasted_iota(jnp.int32, (1, SLOTS), 1)
     picked = jnp.dot(
@@ -136,7 +136,7 @@
         preferred_element_type=jnp.float32,
     )
     value = jnp.sum(jnp.where(second == label, picked, 0.0), axis=0, keepdims=True)
-    keep = (slot < count_ref[0]) & (first != second)
+    keep = (slot < count_ref[...]) & (first != second)
     value = jnp.where(keep, value, 0.0)
     owner = owner_ref[...]
     place = (owner & (NBY - 1)) * NBX + (owner >> 4)
@@ -152,16 +152,25 @@
 
 def whole_kernel(
     f_ref,
-    own_ref,
+    own_hbm,
+    conv_hbm,
+    row_bias_hbm,
+    head_hbm,
+    head_bias_hbm,
+    ends_hbm,
+    owner_hbm,
+    row_hbm,
+    count_hbm,
+    o_ref,
     conv_ref,
-    bias_ref,
+    row_bias_ref,
     head_ref,
     head_bias_ref,
     ends_ref,
     owner_ref,
     row_ref,
     count_ref,
-    o_ref,
+    bias_ref,
     fbuf_ref,
     p_ref,
     lab_ref,
@@ -174,6 +183,7 @@
     got_ref,
     mid_ref,
     last_ref,
+    small_sem,
     load_sem,
     y_send,
     y_recv,
@@ -206,12 +216,37 @@
         at = pl.ds(2 * pair, 2)
         return pltpu.make_async_copy(f_ref.at[:, at], fbuf_ref.at[:, at], load_sem.at[pair])
 
-    for pair in range(CX // 2):
+    small = [
+        pltpu.make_async_copy(src, dst, small_sem.at[n])
+        for n, (src, dst) in enumerate(
+            [
+                (conv_hbm, conv_ref),
+                (own_hbm, lab_ref.at[pl.ds(1, CX)]),
+                (row_bias_hbm, row_bias_ref),
+                (head_hbm, head_ref),
+                (head_bias_hbm, head_bias_ref),
+                (ends_hbm, ends_ref),
+                (owner_hbm, owner_ref),
+                (row_hbm, row_ref),
+                (count_hbm, count_ref),
+            ]
+        )
+    ]
+    for copy in small:
+        copy.start()
+    for pair in (7, 0, 1, 2, 3, 4, 5, 6):
         load(pair).start()
 
-    lab_ref[1:] = own_ref[...]
-    last_line_ref[...] = own_ref[:, CY - 1, :]
     table_ref[...] = jnp.zeros((LABELS, LABELS), jnp.float32)
+    for copy in small:
+        copy.wait()
+    last_line_ref[...] = lab_ref[1:, CY - 1, :]
+    diagonal = lax.broadcasted_iota(jnp.int32, (C, C), 0) == lax.broadcasted_iota(
+        jnp.int32, (C, C), 1
+    )
+    column = jnp.sum(jnp.where(diagonal, row_bias_ref[...], 0.0), axis=1, keepdims=True)
+    for out_y in range(2):
+        bias_ref[out_y * C : (out_y + 1) * C, :] = jnp.broadcast_to(column, (C, CZ))
     lay_weights(conv_ref, w_ref)
     to = lax.broadcasted_iota(jnp.int32, (256, 256), 0)
     come = lax.broadcasted_iota(jnp.int32, (256, 256), 1)
@@ -250,7 +285,7 @@
                 (p_ref.at[CX, inner], p_ref.at[0, inner], (xp, by)),
                 (p_ref.at[CX, 1], p_ref.at[0, CY + 1], (xp, ym)),
                 (p_ref.at[CX, CY], p_ref.at[0, 0], (xp, yp)),
-                (own_ref.at[CX - 1], lab_ref.at[0], (xp, by)),
+                (lab_ref.at[CX], lab_ref.at[0], (xp, by)),
                 (last_line_ref, line_ref, (bx, yp)),
             ]
         )
@@ -355,23 +390,22 @@
     edge_row,
     edge_count,
 ):
-    bias = jnp.broadcast_to(jnp.concatenate([conv_bias, conv_bias])[:, None], (2 * C, CZ))
-    blank = jnp.zeros((3, C), jnp.bfloat16)
-    head = jnp.stack(
-        [
-            jnp.concatenate([head_weight, blank], axis=1),
-            jnp.concatenate([blank, head_weight], axis=1),
-        ],
-        axis=1,
-    ).reshape(6, 2 * C)
-    head = jnp.pad(head, ((0, 10), (0, 0)))
     bf16, f32, i32 = jnp.bfloat16, jnp.float32, jnp.int32
     total = pl.pallas_call(
         whole_kernel,
         out_shape=jax.ShapeDtypeStruct((1, EO), f32),
-        in_specs=[pl.BlockSpec(memory_space=pl.ANY)] + [VMEM] * 4 + [SMEM] + [VMEM] * 3 + [SMEM],
+        in_specs=[pl.BlockSpec(memory_space=pl.ANY)] * 10,
         out_specs=VMEM,
         scratch_shapes=[
+            pltpu.VMEM((C, 27 * C), bf16),
+            pltpu.VMEM((1, C), f32),
+            pltpu.VMEM((3, C), bf16),
+            pltpu.SMEM((3,), f32),
+            pltpu.VMEM((1, 2, SLOTS), i32),
+            pltpu.VMEM((1, SLOTS), i32),
+            pltpu.VMEM((1, SLOTS), i32),
+            pltpu.VMEM((1, 1), i32),
+            pltpu.VMEM((2 * C, CZ), f32),
             pltpu.VMEM((C, CX, CY, CZ), bf16),
             pltpu.VMEM((CX + 2, CY + 2, C, CZ), bf16),
             pltpu.VMEM((CX + 1, CY, CZ), i32),
@@ -384,6 +418,7 @@
             pltpu.VMEM((NBY, NBX, EO), f32),
             pltpu.VMEM((NBX, 1, EO), f32),
             pltpu.VMEM((NBX, 1, EO), f32),
+            pltpu.SemaphoreType.DMA((9,)),
             pltpu.SemaphoreType.DMA((CX // 2,)),
             pltpu.SemaphoreType.DMA((2, CX // 2)),
             pltpu.SemaphoreType.DMA((2, CX // 2)),
@@ -395,20 +430,20 @@
             pltpu.SemaphoreType.DMA((NBX,)),
         ],
         compiler_params=pltpu.CompilerParams(
-            collective_id=0, has_side_effects=True, vmem_limit_bytes=52 * 2**20
+            collective_id=0, has_side_effects=True, vmem_limit_bytes=63 * 2**20
         ),
         name="whole",
     )(
         features,
         labels,
         conv_weight,
-        bias,
-        head,
+        conv_bias[None],
+        head_weight,
         head_bias,
-        edge_ends[0],
+        edge_ends,
         edge_owner[:, :, 0],
         edge_row,
-        edge_count,
+        edge_count[None],
     )
     return total[0]
 

time: 64.2 us -> 58.9 us (0.917)
  local copies, waits for them, and re-layouts: 6 us -> 1.19 us
  other arithmetic: 0.82 us -> 0 us
    unnamed x13 -> x1, local copies, waits for them, and re-layouts: 5.06 us -> 1.19 us
    another operation x2 -> x0, local copies, waits for them, and re-layouts: 0.83 us -> none  [on_device(): jnp.stack([jnp.concatenate([head_weight, blank], axis=1), jnp.concatenate...]
    concatenate x1 -> x0, other arithmetic: 0.81 us -> none  [on_device(): jnp.concatenate([conv_bias, conv_bias])[:, None]]
where the time goes in v3:
time: 58.9 us; the launch traced here: 58.8 us
  Pallas kernels  56.9 us (97%)
  local copies, waits for them, and re-layouts  1.19 us (2%)
  between operations  0.66 us (1%)
    pallas_call x1, Pallas kernels, on_device(): pl.pallas_call(whole_kernel, out_shape=jax.ShapeDtypeStruct((1, EO), f32)...  56.9 us
    unnamed x1, local copies, waits for them, and re-layouts  1.19 us

profile of v3, /device:TPU:1, one launch (start us, length us, event | category | flops | bytes accessed | tf_op | source)
XLA Modules:
  0.0 58.8 jit_solution(17346902681378297600)
XLA Ops:
  0.7 56.9 %whole.1 = f32[1,128]{1,0:T(1,128)} custom-call(bf16[64,16,16,128]{3,2,1,0:T(8,128)(2,1)} %f_ref.1, s32[16,16,128]{2,1,0:T(8,128)} %own_hbm.1, bf16[64,1728]{1,0:T(8,128)(2,1)} %conv_hbm.1, f32[1,64]{1,0:T(1,128)} %bitcast.6, bf16[3,64]{1,0:T(4,128)(2,1)} %head_hbm.1, f32[3]{0:T(128)} %head_bias_hbm.1, s32[1,2,512]{2,1,0:T(2,128)} %ends_hbm.1, ...), custom_call_target="tpu_custom_call" | custom-call | tf_op jit(solution)/shard_map/whole/pallas_call | solution.py:394
  57.6 1.2 %copy.13 = f32[128]{0:T(128)} copy(f32[128]{0:T(128)} %bitcast.7) | data formatting | bytes 1024

commit v4 on v3

--- a/solution.py
+++ b/solution.py
@@ -15,6 +15,8 @@
 C = 64
 SLOTS = 512
 PAIRS = CY // 2
+EARLY = 8
+DEVICES = NBX * NBY
 MESH = pl.DeviceIdType.MESH
 VMEM = pl.BlockSpec(memory_space=pltpu.VMEM)
 
@@ -34,12 +36,12 @@
             )
 
 
-def conv_plane(x, p_ref, w_ref, bias_ref, head_ref, head_bias_ref, logit_ref):
+def conv_pairs(pairs, p_ref, w_ref, bias_ref, head_ref, head_bias_ref, logit_ref):
     lane = lax.broadcasted_iota(jnp.int32, (2 * C, CZ), 1)
     stacked = jnp.concatenate(
         [
             jnp.concatenate(
-                [p_ref[x + dx, 2 * j : 2 * j + 4].reshape(4 * C, CZ) for j in range(PAIRS)], axis=1
+                [p_ref[x + dx, 2 * j : 2 * j + 4].reshape(4 * C, CZ) for x, j in pairs], axis=1
             )
             for dx in range(3)
         ],
@@ -47,8 +49,8 @@
     )
     sums = jnp.dot(w_ref[...], stacked, preferred_element_type=jnp.float32)
     parts = []
-    for j in range(PAIRS):
-        part = sums[:, j * CZ : (j + 1) * CZ]
+    for n in range(len(pairs)):
+        part = sums[:, n * CZ : (n + 1) * CZ]
         before = pltpu.roll(part[: 2 * C], 1, 1)
         after = pltpu.roll(part[4 * C :], CZ - 1, 1)
         pre = (
@@ -61,16 +63,18 @@
     hidden = jnp.concatenate([part[:C] for part in parts] + [part[C:] for part in parts], axis=1)
     logits = jnp.dot(head_ref[...], hidden, preferred_element_type=jnp.float32)
     for d in range(3):
-        for y in range(CY):
-            at = (y % 2) * PAIRS + y // 2
-            logit_ref[d, y : y + 1, :] = (
-                logits[d : d + 1, at * CZ : (at + 1) * CZ] + head_bias_ref[d]
-            )
+        for n, (x, j) in enumerate(pairs):
+            for out_y in range(2):
+                at = out_y * len(pairs) + n
+                y = 2 * j + out_y
+                logit_ref[x, d, y : y + 1, :] = (
+                    logits[d : d + 1, at * CZ : (at + 1) * CZ] + head_bias_ref[d]
+                )
 
 
 def pair_sums(x, logit_ref, lab_ref, line_ref):
     affin = [
-        jax.nn.sigmoid(logit_ref[d]).astype(jnp.bfloat16).astype(jnp.float32) for d in range(3)
+        jax.nn.sigmoid(logit_ref[x, d]).astype(jnp.bfloat16).astype(jnp.float32) for d in range(3)
     ]
     own_i = lab_ref[x + 1]
     line = lax.broadcasted_iota(jnp.int32, (CY, CZ), 0)
@@ -124,30 +128,37 @@
     return found[:LABELS] + found[LABELS:]
 
 
+def two_terms(value, axis):
+    top = value.astype(jnp.bfloat16)
+    rest = (value - top.astype(jnp.float32)).astype(jnp.bfloat16)
+    return jnp.concatenate([top, rest], axis=axis)
+
+
+def one_hot(mask):
+    return jnp.where(mask, 1.0, 0.0).astype(jnp.bfloat16)
+
+
 def slot_rows(table, ends_ref, owner_ref, row_ref, count_ref):
     first = ends_ref[0, 0:1, :]
     second = ends_ref[0, 1:2, :]
     label = lax.broadcasted_iota(jnp.int32, (LABELS, SLOTS), 0)
     slot = lax.broadcasted_iota(jnp.int32, (1, SLOTS), 1)
+    both = table + table.T
     picked = jnp.dot(
-        table + table.T,
-        (first == label).astype(jnp.float32),
-        precision=lax.Precision.HIGHEST,
-        preferred_element_type=jnp.float32,
-    )
+        two_terms(both, 0), one_hot(first == label), preferred_element_type=jnp.float32
+    )
+    picked = picked[:LABELS] + picked[LABELS:]
     value = jnp.sum(jnp.where(second == label, picked, 0.0), axis=0, keepdims=True)
     keep = (slot < count_ref[...]) & (first != second)
     value = jnp.where(keep, value, 0.0)
-    owner = owner_ref[...]
-    place = (owner & (NBY - 1)) * NBX + (owner >> 4)
     row_id = lax.broadcasted_iota(jnp.int32, (EO, SLOTS), 0)
-    return lax.dot_general(
-        jnp.where(place == row_id, value, 0.0),
-        (row_ref[...] == row_id).astype(jnp.float32),
+    spread = lax.dot_general(
+        two_terms(jnp.where(owner_ref[...] == row_id, value, 0.0), 0),
+        one_hot(row_ref[...] == row_id),
         (((1,), (1,)), ((), ())),
-        precision=lax.Precision.HIGHEST,
         preferred_element_type=jnp.float32,
     )
+    return spread[:EO] + spread[EO:]
 
 
 def whole_kernel(
@@ -181,18 +192,14 @@
     table_ref,
     rows_ref,
     got_ref,
-    mid_ref,
-    last_ref,
     small_sem,
     load_sem,
     y_send,
     y_recv,
     x_send,
     x_recv,
-    send1,
-    recv1,
-    send2,
-    recv2,
+    row_send,
+    row_recv,
 ):
     bx = lax.axis_index("bx")
     by = lax.axis_index("by")
@@ -200,17 +207,16 @@
     xp = lax.rem(bx + 1, NBX)
     ym = lax.rem(by + NBY - 1, NBY)
     yp = lax.rem(by + 1, NBY)
+    me = bx * NBY + by
     barrier = pltpu.get_barrier_semaphore()
 
-    def greet(peer):
+    def place_of(flat):
+        return (flat // NBY, lax.rem(flat, NBY))
+
+    def greet(step, carry):
+        peer = place_of(lax.rem(me + step, DEVICES))
         pl.semaphore_signal(barrier, inc=1, device_id=peer, device_id_type=MESH)
-
-    for step in range(1, NBY):
-        greet((bx, lax.rem(by + step, NBY)))
-    for step in range(1, NBX):
-        greet((lax.rem(bx + step, NBX), by))
-    for peer in ((xm, ym), (xm, yp), (xp, ym), (xp, yp)):
-        greet(peer)
+        return carry
 
     def load(pair):
         at = pl.ds(2 * pair, 2)
@@ -237,6 +243,7 @@
     for pair in (7, 0, 1, 2, 3, 4, 5, 6):
         load(pair).start()
 
+    lax.fori_loop(1, DEVICES, greet, 0)
     table_ref[...] = jnp.zeros((LABELS, LABELS), jnp.float32)
     for copy in small:
         copy.wait()
@@ -251,7 +258,7 @@
     to = lax.broadcasted_iota(jnp.int32, (256, 256), 0)
     come = lax.broadcasted_iota(jnp.int32, (256, 256), 1)
     perm = ((to & 15) * 16 + (to >> 4) == come).astype(jnp.float32).astype(jnp.bfloat16)
-    pl.semaphore_wait(barrier, NBX + NBY + 2)
+    pl.semaphore_wait(barrier, DEVICES - 1)
 
     def remote(src, dst, send_sem, recv_sem, peer):
         return pltpu.make_async_remote_copy(
@@ -315,6 +322,13 @@
     for copy in x_copies:
         copy.start()
     lax.fori_loop(2, CX // 2, turned, 0)
+
+    def early(n, carry):
+        pairs = [(1 + 2 * n + m, j) for m in range(2) for j in range(1, PAIRS - 1)]
+        conv_pairs(pairs, p_ref, w_ref, bias_ref, head_ref, head_bias_ref, logit_ref)
+        return carry
+
+    lax.fori_loop(0, EARLY // 2, early, 0)
     for copy in x_copies:
         copy.wait()
     for pair in range(CX // 2):
@@ -339,42 +353,44 @@
     def _():
         p_ref[:, CY + 1] = jnp.zeros((CX + 2, C, CZ), jnp.bfloat16)
 
-    conv_plane(0, p_ref, w_ref, bias_ref, head_ref, head_bias_ref, logit_ref)
-
-    def plane(x, carry):
-        found = pair_sums(x - 1, logit_ref, lab_ref, line_ref)
-        conv_plane(x, p_ref, w_ref, bias_ref, head_ref, head_bias_ref, logit_ref)
+    for half in range(2):
+        pairs = [(1 + 4 * half + n, j) for n in range(4) for j in (0, PAIRS - 1)]
+        conv_pairs(pairs, p_ref, w_ref, bias_ref, head_ref, head_bias_ref, logit_ref)
+
+    def plane(n, carry):
+        x = lax.rem(n + EARLY + 1, CX)
+        found = pair_sums(n + 1, logit_ref, lab_ref, line_ref)
+        pairs = [(x, j) for j in range(PAIRS)]
+        conv_pairs(pairs, p_ref, w_ref, bias_ref, head_ref, head_bias_ref, logit_ref)
         table_ref[...] += found
         return carry
 
-    lax.fori_loop(1, CX, plane, 0)
-    table = table_ref[...] + pair_sums(CX - 1, logit_ref, lab_ref, line_ref)
-    rows_ref[...] = slot_rows(table, ends_ref, owner_ref, row_ref, count_ref).reshape(NBY, NBX, EO)
-
-    copies = []
-    for step in range(1, NBY):
-        to = lax.rem(by + step, NBY)
-        copies.append(
-            remote(rows_ref.at[to], got_ref.at[step], send1.at[step], recv1.at[step], (bx, to))
-        )
-        copies[-1].start()
-    total = rows_ref[by]
-    for step in range(1, NBY):
-        copies[step - 1].wait()
-        total = total + got_ref[step]
-    for row in range(NBX):
-        mid_ref[row] = total[row : row + 1, :]
-    copies = []
-    for step in range(1, NBX):
-        to = lax.rem(bx + step, NBX)
-        copies.append(
-            remote(mid_ref.at[to], last_ref.at[step], send2.at[step], recv2.at[step], (to, by))
-        )
-        copies[-1].start()
-    total = mid_ref[bx]
-    for step in range(1, NBX):
-        copies[step - 1].wait()
-        total = total + last_ref[step]
+    lax.fori_loop(0, CX - EARLY, plane, 0)
+
+    def late(n, carry):
+        x = lax.rem(n + EARLY + 1, CX)
+        table_ref[...] += pair_sums(x, logit_ref, lab_ref, line_ref)
+        return carry
+
+    lax.fori_loop(0, CX - EARLY, late, 0)
+    rows = slot_rows(table_ref[...], ends_ref, owner_ref, row_ref, count_ref)
+    for n in range(EO):
+        rows_ref[n] = rows[n : n + 1, :]
+
+    def give(step, carry):
+        to = lax.rem(me + step, DEVICES)
+        remote(rows_ref.at[to], got_ref.at[step], row_send, row_recv, place_of(to)).start()
+        return carry
+
+    lax.fori_loop(1, DEVICES, give, 0)
+    others = pl.ds(1, DEVICES - 1)
+    remote(
+        rows_ref.at[others], got_ref.at[others], row_send, row_recv, place_of(lax.rem(me + 1, DEVICES))
+    ).wait()
+    totals = [rows_ref[me], got_ref[1], got_ref[2], got_ref[3]]
+    for step in range(4, DEVICES):
+        totals[step % 4] = totals[step % 4] + got_ref[step]
+    total = (totals[0] + totals[1]) + (totals[2] + totals[3])
     o_ref[...] = total
 
 
@@ -412,22 +428,18 @@
             pltpu.VMEM((CX, CZ), i32),
             pltpu.VMEM((CX, CZ), i32),
             pltpu.VMEM((6 * C, 12 * C), bf16),
-            pltpu.VMEM((3, CY, CZ), f32),
+            pltpu.VMEM((CX, 3, CY, CZ), f32),
             pltpu.VMEM((LABELS, LABELS), f32),
-            pltpu.VMEM((NBY, NBX, EO), f32),
-            pltpu.VMEM((NBY, NBX, EO), f32),
-            pltpu.VMEM((NBX, 1, EO), f32),
-            pltpu.VMEM((NBX, 1, EO), f32),
+            pltpu.VMEM((DEVICES, 1, EO), f32),
+            pltpu.VMEM((DEVICES, 1, EO), f32),
             pltpu.SemaphoreType.DMA((9,)),
             pltpu.SemaphoreType.DMA((CX // 2,)),
             pltpu.SemaphoreType.DMA((2, CX // 2)),
             pltpu.SemaphoreType.DMA((2, CX // 2)),
             pltpu.SemaphoreType.DMA((8,)),
             pltpu.SemaphoreType.DMA((8,)),
-            pltpu.SemaphoreType.DMA((NBY,)),
-            pltpu.SemaphoreType.DMA((NBY,)),
-            pltpu.SemaphoreType.DMA((NBX,)),
-            pltpu.SemaphoreType.DMA((NBX,)),
+            pltpu.SemaphoreType.DMA,
+            pltpu.SemaphoreType.DMA,
         ],
         compiler_params=pltpu.CompilerParams(
             collective_id=0, has_side_effects=True, vmem_limit_bytes=63 * 2**20

time: 58.9 us -> 53.7 us (0.912)
  Pallas kernels: 56.9 us -> 51.8 us
    pallas_call x1, Pallas kernels: 56.9 us -> 51.8 us  [on_device(): pl.pallas_call(whole_kernel, out_shape=jax.ShapeDtypeStruct((1, EO), f32)...]
where the time goes in v4:
time: 53.7 us; the launch traced here: 53.6 us
  Pallas kernels  51.8 us (96%)
  local copies, waits for them, and re-layouts  1.19 us (2%)
  between operations  0.66 us (1%)
    pallas_call x1, Pallas kernels, on_device(): pl.pallas_call(whole_kernel, out_shape=jax.ShapeDtypeStruct((1, EO), f32)...  51.8 us
    unnamed x1, local copies, waits for them, and re-layouts  1.19 us

profile of v4, /device:TPU:1, one launch (start us, length us, event | category | flops | bytes accessed | tf_op | source)
XLA Modules:
  0.0 53.6 jit_solution(688981707710622277)
XLA Ops:
  0.7 51.8 %whole.1 = f32[1,128]{1,0:T(1,128)} custom-call(bf16[64,16,16,128]{3,2,1,0:T(8,128)(2,1)} %f_ref.1, s32[16,16,128]{2,1,0:T(8,128)} %own_hbm.1, bf16[64,1728]{1,0:T(8,128)(2,1)} %conv_hbm.1, f32[1,64]{1,0:T(1,128)} %bitcast.6, bf16[3,64]{1,0:T(4,128)(2,1)} %head_hbm.1, f32[3]{0:T(128)} %head_bias_hbm.1, s32[1,2,512]{2,1,0:T(2,128)} %ends_hbm.1, ...), custom_call_target="tpu_custom_call" | custom-call | tf_op jit(solution)/shard_map/whole/pallas_call | solution.py:410
  52.4 1.2 %copy.13 = f32[128]{0:T(128)} copy(f32[128]{0:T(128)} %bitcast.7) | data formatting | bytes 1024

commit v5 on v4

--- a/solution.py
+++ b/solution.py
@@ -36,21 +36,26 @@
             )
 
 
-def conv_pairs(pairs, p_ref, w_ref, bias_ref, head_ref, head_bias_ref, logit_ref):
-    lane = lax.broadcasted_iota(jnp.int32, (2 * C, CZ), 1)
+def conv_dot(pairs, p_ref, w_ref, sums_ref):
     stacked = jnp.concatenate(
         [
             jnp.concatenate(
-                [p_ref[x + dx, 2 * j : 2 * j + 4].reshape(4 * C, CZ) for x, j in pairs], axis=1
+                [p_ref[x + dx, 2 * j : 2 * j + 4].reshape(4 * C, CZ) for x, _, j in pairs], axis=1
             )
             for dx in range(3)
         ],
         axis=0,
     )
-    sums = jnp.dot(w_ref[...], stacked, preferred_element_type=jnp.float32)
+    sums_ref[:, : len(pairs) * CZ] = jnp.dot(
+        w_ref[...], stacked, preferred_element_type=jnp.float32
+    )
+
+
+def conv_head(pairs, sums_ref, bias_ref, head_ref, head_bias_ref, logit_ref):
+    lane = lax.broadcasted_iota(jnp.int32, (2 * C, CZ), 1)
     parts = []
     for n in range(len(pairs)):
-        part = sums[:, n * CZ : (n + 1) * CZ]
+        part = sums_ref[:, n * CZ : (n + 1) * CZ]
         before = pltpu.roll(part[: 2 * C], 1, 1)
         after = pltpu.roll(part[4 * C :], CZ - 1, 1)
         pre = (
@@ -63,18 +68,16 @@
     hidden = jnp.concatenate([part[:C] for part in parts] + [part[C:] for part in parts], axis=1)
     logits = jnp.dot(head_ref[...], hidden, preferred_element_type=jnp.float32)
     for d in range(3):
-        for n, (x, j) in enumerate(pairs):
+        for n, (_, at, j) in enumerate(pairs):
             for out_y in range(2):
-                at = out_y * len(pairs) + n
+                col = (out_y * len(pairs) + n) * CZ
                 y = 2 * j + out_y
-                logit_ref[x, d, y : y + 1, :] = (
-                    logits[d : d + 1, at * CZ : (at + 1) * CZ] + head_bias_ref[d]
-                )
-
-
-def pair_sums(x, logit_ref, lab_ref, line_ref):
+                logit_ref[at, d, y : y + 1, :] = logits[d : d + 1, col : col + CZ] + head_bias_ref[d]
+
+
+def pair_sums(x, at, logit_ref, lab_ref, line_ref):
     affin = [
-        jax.nn.sigmoid(logit_ref[x, d]).astype(jnp.bfloat16).astype(jnp.float32) for d in range(3)
+        jax.nn.sigmoid(logit_ref[at, d]).astype(jnp.bfloat16).astype(jnp.float32) for d in range(3)
     ]
     own_i = lab_ref[x + 1]
     line = lax.broadcasted_iota(jnp.int32, (CY, CZ), 0)
@@ -188,7 +191,10 @@
     line_ref,
     last_line_ref,
     w_ref,
-    logit_ref,
+    logit_a,
+    logit_b,
+    sums_a,
+    sums_b,
     table_ref,
     rows_ref,
     got_ref,
@@ -210,13 +216,21 @@
     me = bx * NBY + by
     barrier = pltpu.get_barrier_semaphore()
 
-    def place_of(flat):
-        return (flat // NBY, lax.rem(flat, NBY))
-
-    def greet(step, carry):
-        peer = place_of(lax.rem(me + step, DEVICES))
-        pl.semaphore_signal(barrier, inc=1, device_id=peer, device_id_type=MESH)
-        return carry
+    lines = [lax.rem(by + step, NBY) for step in range(NBY)]
+
+    def all_peers(visit):
+        def one_x(step, carry):
+            peer_x = lax.rem(bx + step, NBX)
+            for n in range(NBY):
+                visit(peer_x, lines[n], step * NBY + n)
+            return carry
+
+        for n in range(1, NBY):
+            visit(bx, lines[n], n)
+        lax.fori_loop(1, NBX, one_x, 0)
+
+    def greet(peer_x, peer_y, slot):
+        pl.semaphore_signal(barrier, inc=1, device_id=(peer_x, peer_y), device_id_type=MESH)
 
     def load(pair):
         at = pl.ds(2 * pair, 2)
@@ -243,7 +257,7 @@
     for pair in (7, 0, 1, 2, 3, 4, 5, 6):
         load(pair).start()
 
-    lax.fori_loop(1, DEVICES, greet, 0)
+    all_peers(greet)
     table_ref[...] = jnp.zeros((LABELS, LABELS), jnp.float32)
     for copy in small:
         copy.wait()
@@ -323,12 +337,25 @@
         copy.start()
     lax.fori_loop(2, CX // 2, turned, 0)
 
+    def convolve(jobs, logit_ref):
+        for pairs, sums_ref in zip(jobs, (sums_a, sums_b)):
+            conv_dot(pairs, p_ref, w_ref, sums_ref)
+        for pairs, sums_ref in zip(jobs, (sums_a, sums_b)):
+            conv_head(pairs, sums_ref, bias_ref, head_ref, head_bias_ref, logit_ref)
+
     def early(n, carry):
-        pairs = [(1 + 2 * n + m, j) for m in range(2) for j in range(1, PAIRS - 1)]
-        conv_pairs(pairs, p_ref, w_ref, bias_ref, head_ref, head_bias_ref, logit_ref)
+        jobs = [
+            [
+                (1 + 4 * n + 2 * job + m, 4 * n + 2 * job + m, j)
+                for m in range(2)
+                for j in range(1, PAIRS - 1)
+            ]
+            for job in range(2)
+        ]
+        convolve(jobs, logit_a)
         return carry
 
-    lax.fori_loop(0, EARLY // 2, early, 0)
+    lax.fori_loop(0, EARLY // 4, early, 0)
     for copy in x_copies:
         copy.wait()
     for pair in range(CX // 2):
@@ -353,39 +380,47 @@
     def _():
         p_ref[:, CY + 1] = jnp.zeros((CX + 2, C, CZ), jnp.bfloat16)
 
-    for half in range(2):
-        pairs = [(1 + 4 * half + n, j) for n in range(4) for j in (0, PAIRS - 1)]
-        conv_pairs(pairs, p_ref, w_ref, bias_ref, head_ref, head_bias_ref, logit_ref)
+    jobs = [
+        [(1 + 4 * job + m, 4 * job + m, j) for m in range(4) for j in (0, PAIRS - 1)]
+        for job in range(2)
+    ]
+    convolve(jobs, logit_a)
 
     def plane(n, carry):
-        x = lax.rem(n + EARLY + 1, CX)
-        found = pair_sums(n + 1, logit_ref, lab_ref, line_ref)
-        pairs = [(x, j) for j in range(PAIRS)]
-        conv_pairs(pairs, p_ref, w_ref, bias_ref, head_ref, head_bias_ref, logit_ref)
-        table_ref[...] += found
+        late = [2 * n + m for m in range(2)]
+        jobs = [[(lax.rem(k + EARLY + 1, CX), k, j) for j in range(PAIRS)] for k in late]
+        for pairs, sums_ref in zip(jobs, (sums_a, sums_b)):
+            conv_dot(pairs, p_ref, w_ref, sums_ref)
+        found = []
+        for k, pairs, sums_ref in zip(late, jobs, (sums_a, sums_b)):
+            found.append(pair_sums(k + 1, k, logit_a, lab_ref, line_ref))
+            conv_head(pairs, sums_ref, bias_ref, head_ref, head_bias_ref, logit_b)
+        table_ref[...] += found[0] + found[1]
         return carry
 
-    lax.fori_loop(0, CX - EARLY, plane, 0)
+    lax.fori_loop(0, (CX - EARLY) // 2, plane, 0)
 
     def late(n, carry):
-        x = lax.rem(n + EARLY + 1, CX)
-        table_ref[...] += pair_sums(x, logit_ref, lab_ref, line_ref)
+        found = [
+            pair_sums(lax.rem(k + EARLY + 1, CX), k, logit_b, lab_ref, line_ref)
+            for k in (2 * n, 2 * n + 1)
+        ]
+        table_ref[...] += found[0] + found[1]
         return carry
 
-    lax.fori_loop(0, CX - EARLY, late, 0)
+    lax.fori_loop(0, (CX - EARLY) // 2, late, 0)
     rows = slot_rows(table_ref[...], ends_ref, owner_ref, row_ref, count_ref)
     for n in range(EO):
         rows_ref[n] = rows[n : n + 1, :]
 
-    def give(step, carry):
-        to = lax.rem(me + step, DEVICES)
-        remote(rows_ref.at[to], got_ref.at[step], row_send, row_recv, place_of(to)).start()
-        return carry
-
-    lax.fori_loop(1, DEVICES, give, 0)
+    def give(peer_x, peer_y, slot):
+        mine = rows_ref.at[peer_x * NBY + peer_y]
+        remote(mine, got_ref.at[slot], row_send, row_recv, (peer_x, peer_y)).start()
+
+    all_peers(give)
     others = pl.ds(1, DEVICES - 1)
     remote(
-        rows_ref.at[others], got_ref.at[others], row_send, row_recv, place_of(lax.rem(me + 1, DEVICES))
+        rows_ref.at[others], got_ref.at[others], row_send, row_recv, (bx, lines[1])
     ).wait()
     totals = [rows_ref[me], got_ref[1], got_ref[2], got_ref[3]]
     for step in range(4, DEVICES):
@@ -428,7 +463,10 @@
             pltpu.VMEM((CX, CZ), i32),
             pltpu.VMEM((CX, CZ), i32),
             pltpu.VMEM((6 * C, 12 * C), bf16),
-            pltpu.VMEM((CX, 3, CY, CZ), f32),
+            pltpu.VMEM((EARLY, 3, CY, CZ), f32),
+            pltpu.VMEM((CX - EARLY, 3, CY, CZ), f32),
+            pltpu.VMEM((6 * C, 12 * CZ), f32),
+            pltpu.VMEM((6 * C, 12 * CZ), f32),
             pltpu.VMEM((LABELS, LABELS), f32),
             pltpu.VMEM((DEVICES, 1, EO), f32),
             pltpu.VMEM((DEVICES, 1, EO), f32),

time: 53.7 us -> 48.5 us (0.903)
  Pallas kernels: 51.8 us -> 46.5 us
    pallas_call x1, Pallas kernels: 51.8 us -> 46.5 us  [on_device(): pl.pallas_call(whole_kernel, out_shape=jax.ShapeDtypeStruct((1, EO), f32)...]
where the time goes in v5:
time: 48.5 us; the launch traced here: 48.4 us
  Pallas kernels  46.5 us (96%)
  local copies, waits for them, and re-layouts  1.19 us (2%)
  between operations  0.66 us (1%)
    pallas_call x1, Pallas kernels, on_device(): pl.pallas_call(whole_kernel, out_shape=jax.ShapeDtypeStruct((1, EO), f32)...  46.5 us
    unnamed x1, local copies, waits for them, and re-layouts  1.19 us

profile of v5, /device:TPU:1, one launch (start us, length us, event | category | flops | bytes accessed | tf_op | source)
XLA Modules:
  0.0 48.4 jit_solution(9199795001187581532)
XLA Ops:
  0.7 46.5 %whole.1 = f32[1,128]{1,0:T(1,128)} custom-call(bf16[64,16,16,128]{3,2,1,0:T(8,128)(2,1)} %f_ref.1, s32[16,16,128]{2,1,0:T(8,128)} %own_hbm.1, bf16[64,1728]{1,0:T(8,128)(2,1)} %conv_hbm.1, f32[1,64]{1,0:T(1,128)} %bitcast.6, bf16[3,64]{1,0:T(4,128)(2,1)} %head_hbm.1, f32[3]{0:T(128)} %head_bias_hbm.1, s32[1,2,512]{2,1,0:T(2,128)} %ends_hbm.1, ...), custom_call_target="tpu_custom_call" | custom-call | tf_op jit(solution)/shard_map/whole/pallas_call | solution.py:445
  47.2 1.2 %copy.13 = f32[128]{0:T(128)} copy(f32[128]{0:T(128)} %bitcast.7) | data formatting | bytes 1024

commit v6 on v5

--- a/solution.py
+++ b/solution.py
@@ -15,8 +15,10 @@
 C = 64
 SLOTS = 512
 PAIRS = CY // 2
-EARLY = 8
+EARLY = 14
 DEVICES = NBX * NBY
+INNER_ROWS = tuple(range(2, CY - 2))
+BORDER_ROWS = (0, 1, CY - 2, CY - 1)
 MESH = pl.DeviceIdType.MESH
 VMEM = pl.BlockSpec(memory_space=pltpu.VMEM)
 
@@ -75,14 +77,14 @@
                 logit_ref[at, d, y : y + 1, :] = logits[d : d + 1, col : col + CZ] + head_bias_ref[d]
 
 
-def pair_sums(x, at, logit_ref, lab_ref, line_ref):
+def pair_sums(x, at, logit_ref, lab_ref, line_ref, rows=tuple(range(CY))):
     affin = [
         jax.nn.sigmoid(logit_ref[at, d]).astype(jnp.bfloat16).astype(jnp.float32) for d in range(3)
     ]
     own_i = lab_ref[x + 1]
     line = lax.broadcasted_iota(jnp.int32, (CY, CZ), 0)
     deep = lax.broadcasted_iota(jnp.int32, (CY, CZ), 1)
-    edge_line = jnp.broadcast_to(line_ref[pl.ds(x, 1), :], (CY, CZ))
+    edge_line = own_i if line_ref is None else jnp.broadcast_to(line_ref[pl.ds(x, 1), :], (CY, CZ))
     own = own_i.astype(jnp.float32)
     oth_x = lab_ref[x].astype(jnp.float32)
     oth_y = jnp.where(line > 0, pltpu.roll(own_i, 1, 0), edge_line).astype(jnp.float32)
@@ -107,7 +109,7 @@
     zero = jnp.zeros((LABELS, CZ), jnp.bfloat16)
     one = jnp.ones((LABELS, CZ), jnp.bfloat16)
     lefts, tops, rests = [], [], []
-    for y in range(CY):
+    for y in rows:
         lefts.append(jnp.where(spread_row(own, y) == ids, one, zero))
         tops.append(
             jnp.where(
@@ -258,7 +260,6 @@
         load(pair).start()
 
     all_peers(greet)
-    table_ref[...] = jnp.zeros((LABELS, LABELS), jnp.float32)
     for copy in small:
         copy.wait()
     last_line_ref[...] = lab_ref[1:, CY - 1, :]
@@ -343,19 +344,20 @@
         for pairs, sums_ref in zip(jobs, (sums_a, sums_b)):
             conv_head(pairs, sums_ref, bias_ref, head_ref, head_bias_ref, logit_ref)
 
+    def inner_pairs(at):
+        return [(1 + at + m, at + m, j) for m in range(2) for j in range(1, PAIRS - 1)]
+
     def early(n, carry):
-        jobs = [
-            [
-                (1 + 4 * n + 2 * job + m, 4 * n + 2 * job + m, j)
-                for m in range(2)
-                for j in range(1, PAIRS - 1)
-            ]
-            for job in range(2)
-        ]
-        convolve(jobs, logit_a)
+        convolve([inner_pairs(4 * n), inner_pairs(4 * n + 2)], logit_a)
         return carry
 
-    lax.fori_loop(0, EARLY // 4, early, 0)
+    lax.fori_loop(0, (EARLY - 2) // 4, early, 0)
+    conv_dot(inner_pairs(EARLY - 2), p_ref, w_ref, sums_a)
+    found = [
+        pair_sums(at + 1, at, logit_a, lab_ref, None, INNER_ROWS) for at in range(2)
+    ]
+    conv_head(inner_pairs(EARLY - 2), sums_a, bias_ref, head_ref, head_bias_ref, logit_a)
+    table_ref[...] = found[0] + found[1]
     for copy in x_copies:
         copy.wait()
     for pair in range(CX // 2):
@@ -380,35 +382,32 @@
     def _():
         p_ref[:, CY + 1] = jnp.zeros((CX + 2, C, CZ), jnp.bfloat16)
 
+    half = EARLY // 2
     jobs = [
-        [(1 + 4 * job + m, 4 * job + m, j) for m in range(4) for j in (0, PAIRS - 1)]
+        [(1 + half * job + m, half * job + m, j) for m in range(half) for j in (0, PAIRS - 1)]
         for job in range(2)
     ]
     convolve(jobs, logit_a)
 
-    def plane(n, carry):
-        late = [2 * n + m for m in range(2)]
-        jobs = [[(lax.rem(k + EARLY + 1, CX), k, j) for j in range(PAIRS)] for k in late]
-        for pairs, sums_ref in zip(jobs, (sums_a, sums_b)):
-            conv_dot(pairs, p_ref, w_ref, sums_ref)
-        found = []
-        for k, pairs, sums_ref in zip(late, jobs, (sums_a, sums_b)):
-            found.append(pair_sums(k + 1, k, logit_a, lab_ref, line_ref))
-            conv_head(pairs, sums_ref, bias_ref, head_ref, head_bias_ref, logit_b)
+    ends = (CX - 1, 0)
+    jobs = [[(x, k, j) for j in range(PAIRS)] for k, x in enumerate(ends)]
+    for pairs, sums_ref in zip(jobs, (sums_a, sums_b)):
+        conv_dot(pairs, p_ref, w_ref, sums_ref)
+    found = []
+    for at, pairs, sums_ref in zip((2, 3), jobs, (sums_a, sums_b)):
+        found.append(pair_sums(at + 1, at, logit_a, lab_ref, line_ref))
+        conv_head(pairs, sums_ref, bias_ref, head_ref, head_bias_ref, logit_b)
+    table_ref[...] += found[0] + found[1]
+
+    def late(n, carry):
+        found = [pair_sums(k + 1, k, logit_a, lab_ref, line_ref) for k in (2 * n, 2 * n + 1)]
         table_ref[...] += found[0] + found[1]
         return carry
 
-    lax.fori_loop(0, (CX - EARLY) // 2, plane, 0)
-
-    def late(n, carry):
-        found = [
-            pair_sums(lax.rem(k + EARLY + 1, CX), k, logit_b, lab_ref, line_ref)
-            for k in (2 * n, 2 * n + 1)
-        ]
-        table_ref[...] += found[0] + found[1]
-        return carry
-
-    lax.fori_loop(0, (CX - EARLY) // 2, late, 0)
+    lax.fori_loop(2, EARLY // 2, late, 0)
+    found = [pair_sums(x, k, logit_b, lab_ref, line_ref) for k, x in enumerate(ends)]
+    found += [pair_sums(at + 1, at, logit_a, lab_ref, line_ref, BORDER_ROWS) for at in range(2)]
+    table_ref[...] += (found[0] + found[1]) + (found[2] + found[3])
     rows = slot_rows(table_ref[...], ends_ref, owner_ref, row_ref, count_ref)
     for n in range(EO):
         rows_ref[n] = rows[n : n + 1, :]
@@ -465,8 +464,8 @@
             pltpu.VMEM((6 * C, 12 * C), bf16),
             pltpu.VMEM((EARLY, 3, CY, CZ), f32),
             pltpu.VMEM((CX - EARLY, 3, CY, CZ), f32),
-            pltpu.VMEM((6 * C, 12 * CZ), f32),
-            pltpu.VMEM((6 * C, 12 * CZ), f32),
+            pltpu.VMEM((6 * C, EARLY * CZ), f32),
+            pltpu.VMEM((6 * C, EARLY * CZ), f32),
             pltpu.VMEM((LABELS, LABELS), f32),
             pltpu.VMEM((DEVICES, 1, EO), f32),
             pltpu.VMEM((DEVICES, 1, EO), f32),

time: 48.5 us -> 45.7 us (0.942)
  Pallas kernels: 46.5 us -> 43.7 us
    pallas_call x1, Pallas kernels: 46.5 us -> 43.7 us  [on_device(): pl.pallas_call(whole_kernel, out_shape=jax.ShapeDtypeStruct((1, EO), f32)...]
where the time goes in v6:
time: 45.7 us; the launch traced here: 45.6 us
  Pallas kernels  43.7 us (96%)
  local copies, waits for them, and re-layouts  1.19 us (3%)
  between operations  0.66 us (1%)
    pallas_call x1, Pallas kernels, on_device(): pl.pallas_call(whole_kernel, out_shape=jax.ShapeDtypeStruct((1, EO), f32)...  43.7 us
    unnamed x1, local copies, waits for them, and re-layouts  1.19 us

profile of v6, /device:TPU:1, one launch (start us, length us, event | category | flops | bytes accessed | tf_op | source)
XLA Modules:
  0.0 45.6 jit_solution(7218800134730492712)
XLA Ops:
  0.7 43.7 %whole.1 = f32[1,128]{1,0:T(1,128)} custom-call(bf16[64,16,16,128]{3,2,1,0:T(8,128)(2,1)} %f_ref.1, s32[16,16,128]{2,1,0:T(8,128)} %own_hbm.1, bf16[64,1728]{1,0:T(8,128)(2,1)} %conv_hbm.1, f32[1,64]{1,0:T(1,128)} %bitcast.6, bf16[3,64]{1,0:T(4,128)(2,1)} %head_hbm.1, f32[3]{0:T(128)} %head_bias_hbm.1, s32[1,2,512]{2,1,0:T(2,128)} %ends_hbm.1, ...), custom_call_target="tpu_custom_call" | custom-call | tf_op jit(solution)/shard_map/whole/pallas_call | solution.py:444
  44.4 1.2 %copy.13 = f32[128]{0:T(128)} copy(f32[128]{0:T(128)} %bitcast.7) | data formatting | bytes 1024

commit v7 on v6

--- a/solution.py
+++ b/solution.py
@@ -1,3 +1,5 @@
+import functools
+
 import jax
 import jax.numpy as jnp
 from jax import lax
@@ -16,6 +18,7 @@
 SLOTS = 512
 PAIRS = CY // 2
 EARLY = 14
+INNER = 6
 DEVICES = NBX * NBY
 INNER_ROWS = tuple(range(2, CY - 2))
 BORDER_ROWS = (0, 1, CY - 2, CY - 1)
@@ -313,9 +316,7 @@
         )
     ]
 
-    def turned(n, carry):
-        pair = lax.rem(n + CX // 2 - 1, CX // 2)
-        load(pair).wait()
+    def turn(pair):
         for group in range(C // 16):
             block = jnp.concatenate(
                 [
@@ -329,6 +330,11 @@
                 p_ref[1 + 2 * pair + half, 1 : CY + 1, 16 * group : 16 * group + 16, :] = out[
                     :, half * CZ : (half + 1) * CZ
                 ].reshape(CY, 16, CZ)
+
+    def turned(n, carry):
+        pair = lax.rem(n + CX // 2 - 1, CX // 2)
+        load(pair).wait()
+        turn(pair)
         for copy in y_copies(pair):
             copy.start()
         return carry
@@ -336,7 +342,7 @@
     lax.fori_loop(0, 2, turned, 0)
     for copy in x_copies:
         copy.start()
-    lax.fori_loop(2, CX // 2, turned, 0)
+    lax.fori_loop(2, 3, turned, 0)
 
     def convolve(jobs, logit_ref):
         for pairs, sums_ref in zip(jobs, (sums_a, sums_b)):
@@ -348,16 +354,32 @@
         return [(1 + at + m, at + m, j) for m in range(2) for j in range(1, PAIRS - 1)]
 
     def early(n, carry):
-        convolve([inner_pairs(4 * n), inner_pairs(4 * n + 2)], logit_a)
+        load(n + 2).wait()
+        conv_dot(inner_pairs(2 * n), p_ref, w_ref, sums_a)
+        turn(n + 2)
+        conv_head(inner_pairs(2 * n), sums_a, bias_ref, head_ref, head_bias_ref, logit_a)
+        for copy in y_copies(n + 2):
+            copy.start()
         return carry
 
-    lax.fori_loop(0, (EARLY - 2) // 4, early, 0)
-    conv_dot(inner_pairs(EARLY - 2), p_ref, w_ref, sums_a)
-    found = [
-        pair_sums(at + 1, at, logit_a, lab_ref, None, INNER_ROWS) for at in range(2)
-    ]
-    conv_head(inner_pairs(EARLY - 2), sums_a, bias_ref, head_ref, head_bias_ref, logit_a)
+    lax.fori_loop(0, CX // 2 - 3, early, 0)
+    jobs = (inner_pairs(EARLY - 4), inner_pairs(EARLY - 2))
+    for pairs, sums_ref in zip(jobs, (sums_a, sums_b)):
+        conv_dot(pairs, p_ref, w_ref, sums_ref)
+    found = []
+    for at, pairs, sums_ref in zip(range(2), jobs, (sums_a, sums_b)):
+        found.append(pair_sums(at + 1, at, logit_a, lab_ref, None, INNER_ROWS))
+        conv_head(pairs, sums_ref, bias_ref, head_ref, head_bias_ref, logit_a)
     table_ref[...] = found[0] + found[1]
+
+    def inner_sums(n, carry):
+        found = [
+            pair_sums(at + 1, at, logit_a, lab_ref, None, INNER_ROWS) for at in (2 * n, 2 * n + 1)
+        ]
+        table_ref[...] += found[0] + found[1]
+        return carry
+
+    lax.fori_loop(1, INNER // 2, inner_sums, 0)
     for copy in x_copies:
         copy.wait()
     for pair in range(CX // 2):
@@ -383,18 +405,22 @@
         p_ref[:, CY + 1] = jnp.zeros((CX + 2, C, CZ), jnp.bfloat16)
 
     half = EARLY // 2
-    jobs = [
-        [(1 + half * job + m, half * job + m, j) for m in range(half) for j in (0, PAIRS - 1)]
-        for job in range(2)
-    ]
-    convolve(jobs, logit_a)
+
+    def border(job, carry):
+        at = half * job
+        pairs = [(1 + at + m, at + m, j) for m in range(half) for j in (0, PAIRS - 1)]
+        conv_dot(pairs, p_ref, w_ref, sums_a)
+        conv_head(pairs, sums_a, bias_ref, head_ref, head_bias_ref, logit_a)
+        return carry
+
+    lax.fori_loop(0, 2, border, 0)
 
     ends = (CX - 1, 0)
     jobs = [[(x, k, j) for j in range(PAIRS)] for k, x in enumerate(ends)]
     for pairs, sums_ref in zip(jobs, (sums_a, sums_b)):
         conv_dot(pairs, p_ref, w_ref, sums_ref)
     found = []
-    for at, pairs, sums_ref in zip((2, 3), jobs, (sums_a, sums_b)):
+    for at, pairs, sums_ref in zip((INNER, INNER + 1), jobs, (sums_a, sums_b)):
         found.append(pair_sums(at + 1, at, logit_a, lab_ref, line_ref))
         conv_head(pairs, sums_ref, bias_ref, head_ref, head_bias_ref, logit_b)
     table_ref[...] += found[0] + found[1]
@@ -404,10 +430,10 @@
         table_ref[...] += found[0] + found[1]
         return carry
 
-    lax.fori_loop(2, EARLY // 2, late, 0)
+    lax.fori_loop(INNER // 2 + 1, EARLY // 2, late, 0)
     found = [pair_sums(x, k, logit_b, lab_ref, line_ref) for k, x in enumerate(ends)]
-    found += [pair_sums(at + 1, at, logit_a, lab_ref, line_ref, BORDER_ROWS) for at in range(2)]
-    table_ref[...] += (found[0] + found[1]) + (found[2] + found[3])
+    found += [pair_sums(at + 1, at, logit_a, lab_ref, line_ref, BORDER_ROWS) for at in range(INNER)]
+    table_ref[...] += functools.reduce(jnp.add, found)
     rows = slot_rows(table_ref[...], ends_ref, owner_ref, row_ref, count_ref)
     for n in range(EO):
         rows_ref[n] = rows[n : n + 1, :]

time: 45.7 us -> 45 us (0.985)
  Pallas kernels: 43.7 us -> 43 us
    pallas_call x1, Pallas kernels: 43.7 us -> 43 us  [on_device(): pl.pallas_call(whole_kernel, out_shape=jax.ShapeDtypeStruct((1, EO), f32)...]
where the time goes in v7:
time: 45 us; the launch traced here: 44.9 us
  Pallas kernels  43 us (96%)
  local copies, waits for them, and re-layouts  1.19 us (3%)
  between operations  0.66 us (1%)
    pallas_call x1, Pallas kernels, on_device(): pl.pallas_call(whole_kernel, out_shape=jax.ShapeDtypeStruct((1, EO), f32)...  43 us
    unnamed x1, local copies, waits for them, and re-layouts  1.19 us

profile of v7, /device:TPU:1, one launch (start us, length us, event | category | flops | bytes accessed | tf_op | source)
XLA Modules:
  0.0 44.9 jit_solution(175428410991283957)
XLA Ops:
  0.7 43.0 %whole.1 = f32[1,128]{1,0:T(1,128)} custom-call(bf16[64,16,16,128]{3,2,1,0:T(8,128)(2,1)} %f_ref.1, s32[16,16,128]{2,1,0:T(8,128)} %own_hbm.1, bf16[64,1728]{1,0:T(8,128)(2,1)} %conv_hbm.1, f32[1,64]{1,0:T(1,128)} %bitcast.6, bf16[3,64]{1,0:T(4,128)(2,1)} %head_hbm.1, f32[3]{0:T(128)} %head_bias_hbm.1, s32[1,2,512]{2,1,0:T(2,128)} %ends_hbm.1, ...), custom_call_target="tpu_custom_call" | custom-call | tf_op jit(solution)/shard_map/whole/pallas_call | solution.py:470
  43.7 1.2 %copy.13 = f32[128]{0:T(128)} copy(f32[128]{0:T(128)} %bitcast.7) | data formatting | bytes 1024

commit v8 on v7

--- a/solution.py
+++ b/solution.py
@@ -276,7 +276,6 @@
     to = lax.broadcasted_iota(jnp.int32, (256, 256), 0)
     come = lax.broadcasted_iota(jnp.int32, (256, 256), 1)
     perm = ((to & 15) * 16 + (to >> 4) == come).astype(jnp.float32).astype(jnp.bfloat16)
-    pl.semaphore_wait(barrier, DEVICES - 1)
 
     def remote(src, dst, send_sem, recv_sem, peer):
         return pltpu.make_async_remote_copy(
@@ -335,14 +334,15 @@
         pair = lax.rem(n + CX // 2 - 1, CX // 2)
         load(pair).wait()
         turn(pair)
+        return carry
+
+    lax.fori_loop(0, 3, turned, 0)
+    pl.semaphore_wait(barrier, DEVICES - 1)
+    for pair in (CX // 2 - 1, 0, 1):
         for copy in y_copies(pair):
             copy.start()
-        return carry
-
-    lax.fori_loop(0, 2, turned, 0)
     for copy in x_copies:
         copy.start()
-    lax.fori_loop(2, 3, turned, 0)
 
     def convolve(jobs, logit_ref):
         for pairs, sums_ref in zip(jobs, (sums_a, sums_b)):

time: 45 us -> 44 us (0.978)
  Pallas kernels: 43 us -> 42.1 us
    pallas_call x1, Pallas kernels: 43 us -> 42.1 us  [on_device(): pl.pallas_call(whole_kernel, out_shape=jax.ShapeDtypeStruct((1, EO), f32)...]
where the time goes in v8:
time: 44 us; the launch traced here: 43.9 us
  Pallas kernels  42.1 us (96%)
  local copies, waits for them, and re-layouts  1.19 us (3%)
  between operations  0.66 us (2%)
    pallas_call x1, Pallas kernels, on_device(): pl.pallas_call(whole_kernel, out_shape=jax.ShapeDtypeStruct((1, EO), f32)...  42.1 us
    unnamed x1, local copies, waits for them, and re-layouts  1.19 us

profile of v8, /device:TPU:1, one launch (start us, length us, event | category | flops | bytes accessed | tf_op | source)
XLA Modules:
  0.0 43.9 jit_solution(2471118612695814747)
XLA Ops:
  0.7 42.1 %whole.1 = f32[1,128]{1,0:T(1,128)} custom-call(bf16[64,16,16,128]{3,2,1,0:T(8,128)(2,1)} %f_ref.1, s32[16,16,128]{2,1,0:T(8,128)} %own_hbm.1, bf16[64,1728]{1,0:T(8,128)(2,1)} %conv_hbm.1, f32[1,64]{1,0:T(1,128)} %bitcast.6, bf16[3,64]{1,0:T(4,128)(2,1)} %head_hbm.1, f32[3]{0:T(128)} %head_bias_hbm.1, s32[1,2,512]{2,1,0:T(2,128)} %ends_hbm.1, ...), custom_call_target="tpu_custom_call" | custom-call | tf_op jit(solution)/shard_map/whole/pallas_call | solution.py:470
  42.7 1.2 %copy.13 = f32[128]{0:T(128)} copy(f32[128]{0:T(128)} %bitcast.7) | data formatting | bytes 1024
